TPU v7x, 32 devices: a whole 2x2x4 slice. The times are simulated.
32 devices in a mesh: cuts: 4 (over y, x), layer: 8 (over z, core).
Axes of the slice: x: 2, y: 2, z: 4, core: 2. Of those that a mesh axis runs over, the one named last changes fastest.
Arguments:
- vectors: float32 [4, 64, 16, 1024], P('cuts', None, 'layer'), may hold values from -40 to 40
- diag_blocks: bfloat16 [16, 1024, 1024], P('layer'), may hold values from -1 to 1, as said below
- couplings: bfloat16 [16, 1024, 1024], P('layer'), may hold values from -0.09375 to 0.09375
- bounds: int32 [4, 2], P('cuts'), may hold values from -128 to 160, as said below
Outputs:
- filtered: float32 [4, 64, 16, 1024], P('cuts', None, 'layer')
Inputs may be any that keep to these rules, and one draw needn't show every extreme that they name: `bounds`: column 0 holds each slice's lower end, which is -128 at slice 0 and to at most -81; column 1 holds its upper end, from 128 to 160. `diag_blocks`: each block is symmetric.
All inputs are finite; a program needn't handle non-finite values.
Results may differ from a plain program's by a relative error of at most 0.012.
Values may be sent and summed in bfloat16 or wider, within the bound.
No kernel may reach another device: no remote copies, remote signals or barrier semaphores. Data moves between devices by JAX's collectives and lax.ppermute only.
A program may use at most 64 MiB of HBM per device.

v0:
```python
import jax
import jax.numpy as jnp
from jax import lax
from jax.sharding import PartitionSpec as P

EDGE = 16
DEG = 4


def shifted(block, axis, distance):
    devices = range(lax.axis_size(axis))
    route = [(i - distance, i) for i in devices if i - distance in devices]
    return lax.ppermute(block, axis, route)


def inner_products(first, second):
    return jnp.einsum("kn,jn->kj", first, second, precision=lax.Precision.HIGHEST)


def left_solve(factor, right_side):
    return lax.linalg.triangular_solve(factor, right_side, left_side=True, lower=True)


def per_device(vectors, diag_blocks, couplings, bounds):
    current_block = vectors[0]
    count_vec, layers, width = current_block.shape
    length_all = lax.axis_size("layer") * layers * width
    bottom = bounds[0, 0].astype(jnp.float32) / 64.0
    summit = bounds[0, 1].astype(jnp.float32) / 64.0
    centre = (bottom + summit) / 2.0
    half_width = (summit - bottom) / 2.0

    def apply_operator(vectors_now):
        rounded = vectors_now.astype(jnp.bfloat16)
        arrived_first = shifted(rounded[:, :1], "layer", -1)
        following = jnp.concatenate([rounded[:, 1:], arrived_first], 1)
        tail_term = jnp.einsum(
            "kd,de->ke",
            rounded[:, layers - 1],
            couplings[layers - 1],
            preferred_element_type=jnp.float32,
        )
        arrived_tail = shifted(tail_term[:, None], "layer", 1)
        inner_term = jnp.einsum(
            "kld,lde->kle",
            rounded[:, : layers - 1],
            couplings[: layers - 1],
            preferred_element_type=jnp.float32,
        )
        result = jnp.einsum(
            "kld,lde->kle", rounded, diag_blocks, preferred_element_type=jnp.float32
        )
        result = result + jnp.einsum(
            "kle,lde->kld", following, couplings, preferred_element_type=jnp.float32
        )
        return result + jnp.concatenate([arrived_tail, inner_term], 1)

    def filter_block(start):
        previous = start
        current = (apply_operator(start) - centre * start) / half_width
        for degree_index in range(DEG - 1):
            following = 2.0 * (apply_operator(current) - centre * current) / half_width - previous
            previous = current
            current = following
        return current

    def orthonormal(filtered):
        flat = filtered.reshape(count_vec, layers * width)
        gram = lax.psum(inner_products(flat, flat), "layer") / length_all
        return left_solve(jnp.linalg.cholesky(gram), flat)

    current_block = orthonormal(filter_block(current_block)).reshape(count_vec, layers, width)
    filtered = filter_block(current_block)
    final = orthonormal(filtered)
    low_edge = final[:EDGE]
    high_edge = final[count_vec - EDGE :]
    below_high = shifted(high_edge.astype(jnp.bfloat16), "cuts", 1).astype(high_edge.dtype)
    above_low = shifted(low_edge.astype(jnp.bfloat16), "cuts", -1).astype(low_edge.dtype)
    correlation_low, correlation_high = lax.psum(
        (inner_products(below_high, low_edge), inner_products(above_low, high_edge)), "layer"
    )
    low_new = low_edge - jnp.einsum(
        "wv,wn->vn", correlation_low / length_all, below_high, precision=lax.Precision.HIGHEST
    )
    high_new = high_edge - jnp.einsum(
        "wv,wn->vn", correlation_high / length_all, above_low, precision=lax.Precision.HIGHEST
    )
    result = jnp.concatenate([low_new, final[EDGE : count_vec - EDGE], high_new], 0)
    return result.reshape(1, count_vec, layers, width)


def solution(mesh):
    in_specs = (
        P("cuts", None, "layer", None),
        P("layer", None, None),
        P("layer", None, None),
        P("cuts", None),
    )
    out_specs = P("cuts", None, "layer", None)
    return jax.shard_map(
        per_device, mesh=mesh, in_specs=in_specs, out_specs=out_specs, check_vma=False
    )
```

profile of v0, /device:TPU:0, one launch (start us, length us, event | category | flops | bytes accessed | tf_op | source)
XLA Modules:
  0.0 211.7 jit_solution(6247043407058147539)
XLA Ops:
  0.0 1.2 copy.34
  1.2 1.6 collective-permute-start
  2.8 2.1 fusion.76
  4.9 3.2 %collective-permute-start.1 = (f32[64,1,1024]{2,0,1:T(8,128)S(1)}, f32[64,1,1024]{2,0,1:T(8,128)S(1)}, u32[]{:S(2)}, u32[]{:S(2)}) collective-permute-start(f32[64,1,1024]{2,0,1:T(8,128)S(1)} %fusion.76), channel_id=1, source_target_pairs={{0,1},{1,2},{2,3},{3,4},{4,5},{5,6},{6,7},{8,9},{9,10},{10,11},{11... | collective-permute-start | bytes 786440 | tf_op jit(solution)/shard_map/ppermute | solution.py:13
  8.1 3.0 %convolution_bitcast_fusion = f32[64,2,1024]{2,0,1:T(8,128)S(1)} fusion(bf16[64,2,1024]{2,0,1:T(8,128)(2,1)S(1)} %bitcast.352, bf16[2,1024,1024]{2,1,0:T(8,128)(2,1)} %param.8), kind=kOutput, calls=%fused_computation.34 | convolution fusion | flops 268435456 | bytes 4980736 | tf_op jit(solution)/shard_map/kld,lde->kle/dot_general | solution.py:50
  11.1 0.6 fusion.233
  13.5 1.5 fusion.234
  15.7 0.9 fusion.240
  16.5 4.5 %collective-permute-start.3 = (f32[64,1,1024]{2,0,1:T(8,128)S(1)}, f32[64,1,1024]{2,0,1:T(8,128)S(1)}, u32[]{:S(2)}, u32[]{:S(2)}) collective-permute-start(f32[64,1,1024]{2,0,1:T(8,128)S(1)} %fusion.79), channel_id=1, source_target_pairs={{0,1},{1,2},{2,3},{3,4},{4,5},{5,6},{6,7},{8,9},{9,10},{10,11},{11... | collective-permute-start | bytes 786440 | tf_op jit(solution)/shard_map/ppermute | solution.py:13
  21.1 1.3 collective-permute-start.2
  22.9 1.5 collective-permute-done.2
  24.4 1.5 fusion.235
  26.4 0.8 fusion.241
  27.2 5.5 %collective-permute-start.5 = (f32[64,1,1024]{2,0,1:T(8,128)S(1)}, f32[64,1,1024]{2,0,1:T(8,128)S(1)}, u32[]{:S(2)}, u32[]{:S(2)}) collective-permute-start(f32[64,1,1024]{2,0,1:T(8,128)S(1)} %fusion.82), channel_id=1, source_target_pairs={{0,1},{1,2},{2,3},{3,4},{4,5},{5,6},{6,7},{8,9},{9,10},{10,11},{11... | collective-permute-start | bytes 786440 | tf_op jit(solution)/shard_map/ppermute | solution.py:13
  32.7 1.3 collective-permute-start.4
  34.5 1.5 collective-permute-done.4
  35.9 1.4 fusion.236
  37.9 0.8 fusion.242
  38.7 5.0 %collective-permute-start.7 = (f32[64,1,1024]{2,0,1:T(8,128)S(1)}, f32[64,1,1024]{2,0,1:T(8,128)S(1)}, u32[]{:S(2)}, u32[]{:S(2)}) collective-permute-start(f32[64,1,1024]{2,0,1:T(8,128)S(1)} %fusion.85), channel_id=1, source_target_pairs={{0,1},{1,2},{2,3},{3,4},{4,5},{5,6},{6,7},{8,9},{9,10},{10,11},{11... | collective-permute-start | bytes 786440 | tf_op jit(solution)/shard_map/ppermute | solution.py:13
  43.7 1.3 collective-permute-start.6
  45.5 1.5 collective-permute-done.6
  46.9 1.4 fusion.69
  48.4 0.6 convolution_bitcast_fusion.3
  48.9 28.9 %psum.28 = f32[64,64]{0,1:T(8,128)S(1)} all-reduce(f32[64,64]{0,1:T(8,128)S(1)} %convolution_bitcast_fusion.3), channel_id=1, replica_groups=mesh['cuts'=4,'layer'=8] {'layer'}, use_global_device_ids=true, to_apply=%region_0.0 | all-reduce | flops 4096 | bytes 32768 | tf_op jit(solution)/shard_map/psum | solution.py:69
  77.9 5.8 %cholesky.44 = f32[64,64]{1,0:T(8,128)S(1)} custom-call(f32[64,64]{1,0:T(8,128)S(1)} %fusion.191), custom_call_target="Cholesky" | custom-call | tf_op jit(solution)/shard_map/jit(cholesky)/cholesky | solution.py:70
  83.8 0.7 compare_reduce_fusion.1
  84.5 0.6 fusion.184
  85.1 4.9 %custom-call.6 = f32[1,64,64]{1,2,0:T(8,128)S(1)} custom-call(f32[1,64,64]{2,1,0:T(8,128)S(1)} %fusion.184), custom_call_target="InvertDiagBlocksLowerTriangular" | custom-call | tf_op jit(solution)/shard_map/triangular_solve/custom-call.0 | solution.py:21
  90.1 0.6 fusion.189
  90.7 2.4 %fusion.88 = f32[64,1,1024]{2,0,1:T(8,128)S(1)} fusion(bf16[2,1024,1024]{2,1,0:T(8,128)(2,1)} %param.9, bf16[64,2,1024]{2,0,1:T(8,128)(2,1)S(1)} %bitcast.354), kind=kOutput, calls=%fused_computation.91 | convolution fusion | flops 134217728 | bytes 2490368 | tf_op jit(solution)/shard_map/kd,de->ke/dot_general | solution.py:37
  93.2 0.9 fusion.243
  94.0 1.3 collective-permute-start.9
  95.4 1.3 collective-permute-start.8
  97.2 1.4 collective-permute-done.8
  98.6 1.4 fusion.237
  100.1 0.5 fusion.91
  100.6 0.9 fusion.244
  101.4 3.6 %collective-permute-start.11 = (f32[64,1,1024]{2,0,1:T(8,128)S(1)}, f32[64,1,1024]{2,0,1:T(8,128)S(1)}, u32[]{:S(2)}, u32[]{:S(2)}) collective-permute-start(f32[64,1,1024]{2,0,1:T(8,128)S(1)} %fusion.91), channel_id=1, source_target_pairs={{0,1},{1,2},{2,3},{3,4},{4,5},{5,6},{6,7},{8,9},{9,10},{10,11},{11... | collective-permute-start | bytes 786440 | tf_op jit(solution)/shard_map/ppermute | solution.py:13
  105.1 1.3 collective-permute-start.10
  106.9 1.5 collective-permute-done.10
  108.4 1.4 fusion.238
  110.3 0.8 fusion.245
  111.1 5.0 %collective-permute-start.13 = (f32[64,1,1024]{2,0,1:T(8,128)S(1)}, f32[64,1,1024]{2,0,1:T(8,128)S(1)}, u32[]{:S(2)}, u32[]{:S(2)}) collective-permute-start(f32[64,1,1024]{2,0,1:T(8,128)S(1)} %fusion.94), channel_id=1, source_target_pairs={{0,1},{1,2},{2,3},{3,4},{4,5},{5,6},{6,7},{8,9},{9,10},{10,11},{11... | collective-permute-start | bytes 786440 | tf_op jit(solution)/shard_map/ppermute | solution.py:13
  116.1 1.3 collective-permute-start.12
  117.9 1.5 collective-permute-done.12
  119.4 1.4 fusion.239
  121.3 0.8 fusion.246
  122.1 5.0 %collective-permute-start.15 = (f32[64,1,1024]{2,0,1:T(8,128)S(1)}, f32[64,1,1024]{2,0,1:T(8,128)S(1)}, u32[]{:S(2)}, u32[]{:S(2)}) collective-permute-start(f32[64,1,1024]{2,0,1:T(8,128)S(1)} %fusion.97), channel_id=1, source_target_pairs={{0,1},{1,2},{2,3},{3,4},{4,5},{5,6},{6,7},{8,9},{9,10},{10,11},{11... | collective-permute-start | bytes 786440 | tf_op jit(solution)/shard_map/ppermute | solution.py:13
  127.1 1.5 collective-permute-start.14
  129.1 1.2 collective-permute-done.14
  130.4 1.4 fusion.75
  131.8 0.6 convolution_bitcast_fusion.2
  132.4 28.8 %psum.29 = f32[64,64]{0,1:T(8,128)S(1)} all-reduce(f32[64,64]{0,1:T(8,128)S(1)} %convolution_bitcast_fusion.2), channel_id=1, replica_groups=mesh['cuts'=4,'layer'=8] {'layer'}, use_global_device_ids=true, to_apply=%region_3.6 | all-reduce | flops 4096 | bytes 32768 | tf_op jit(solution)/shard_map/psum | solution.py:69
  161.3 5.8 %cholesky.55 = f32[64,64]{1,0:T(8,128)S(1)} custom-call(f32[64,64]{1,0:T(8,128)S(1)} %fusion.188), custom_call_target="Cholesky" | custom-call | tf_op jit(solution)/shard_map/jit(cholesky)/cholesky | solution.py:70
  167.2 0.6 compare_reduce_fusion
  167.8 0.7 fusion.185
  168.5 4.9 %custom-call.7 = f32[1,64,64]{1,2,0:T(8,128)S(1)} custom-call(f32[1,64,64]{2,1,0:T(8,128)S(1)} %fusion.185), custom_call_target="InvertDiagBlocksLowerTriangular" | custom-call | tf_op jit(solution)/shard_map/triangular_solve/custom-call.0 | solution.py:21
  173.4 0.6 fusion.186
  174.1 3.4 %collective-permute-start.16 = (bf16[16,2048]{1,0:T(8,128)(2,1)S(1)}, bf16[16,2048]{1,0:T(8,128)(2,1)S(1)}, u32[]{:S(2)}, u32[]{:S(2)}) collective-permute-start(bf16[16,2048]{1,0:T(8,128)(2,1)S(1)} %get-tuple-element.9), channel_id=1, source_target_pairs={{0,8},{8,16},{16,24},{1,9},{9,17},{17,25},{2,10},{10,18},{18,26},{... | collective-permute-start | bytes 196616 | tf_op jit(solution)/shard_map/ppermute | solution.py:13
  177.5 1.3 collective-permute-start.17
  178.8 0.6 collective-permute-done.16
  179.6 4.1 %collective-permute-done.17 = bf16[16,2048]{1,0:T(8,128)(2,1)S(1)} collective-permute-done((bf16[16,2048]{1,0:T(8,128)(2,1)S(1)}, bf16[16,2048]{1,0:T(8,128)(2,1)S(1)}, u32[]{:S(2)}, u32[]{:S(2)}) %collective-permute-start.17) | collective-permute-done | bytes 65568 | tf_op jit(solution)/shard_map/ppermute | solution.py:13
  183.9 26.0 %all-reduce = (f32[16,16]{1,0:T(8,128)S(1)}, f32[16,16]{1,0:T(8,128)S(1)}) all-reduce(f32[16,16]{1,0:T(8,128)S(1)} %fusion.180, f32[16,16]{1,0:T(8,128)S(1)} %fusion.182), channel_id=1, replica_groups=mesh['cuts'=4,'layer'=8] {'layer'}, use_global_device_ids=true, to_apply=%region_5.8 | all-reduce | flops 512 | bytes 4096 | tf_op jit(solution)/shard_map/psum | solution.py:79
  210.4 1.2 reshape.89
  (60 shorter events, 7.9 us)
Async XLA Ops:
  1.2 9.9 %copy-start.5 = (s32[1,2]{1,0:T(1,128)S(1)}, s32[1,2]{1,0:T(1,128)}, u32[]{:S(2)}) copy-start(s32[1,2]{1,0:T(1,128)} %param.10) | copy-start | bytes 28
  1.2 11.7 %copy-start.2 = (bf16[2,1024,1024]{2,1,0:T(8,128)(2,1)S(1)}, bf16[2,1024,1024]{2,1,0:T(8,128)(2,1)}, u32[]{:S(2)}) copy-start(bf16[2,1024,1024]{2,1,0:T(8,128)(2,1)} %param.9) | copy-start | bytes 12582916
  1.2 12.2 %collective-permute-start = (bf16[64,1,1024]{2,0,1:T(8,128)(2,1)S(1)}, bf16[64,1,1024]{2,0,1:T(8,128)(2,1)S(1)}, u32[]{:S(2)}, u32[]{:S(2)}) collective-permute-start(bf16[64,1,1024]{2,0,1:T(8,128)(2,1)S(1)} %get-tuple-element.26), channel_id=1, source_target_pairs={{1,0},{2,1},{3,2},{4,3},{5,4},{6,5},{7,6},{9,8},{10,9},{11,10},{12... | collective-permute-start | bytes 393224 | tf_op jit(solution)/shard_map/ppermute | solution.py:13
  4.9 8.6 %copy-start.4 = (f32[1,64,2,1024]{3,2,1,0:T(2,128)S(1)}, f32[1,64,2,1024]{3,2,1,0:T(2,128)}, u32[]{:S(2)}) copy-start(f32[1,64,2,1024]{3,2,1,0:T(2,128)} %param.7) | copy-start | bytes 1572868
  4.9 8.6 %collective-permute-start.1 = (f32[64,1,1024]{2,0,1:T(8,128)S(1)}, f32[64,1,1024]{2,0,1:T(8,128)S(1)}, u32[]{:S(2)}, u32[]{:S(2)}) collective-permute-start(f32[64,1,1024]{2,0,1:T(8,128)S(1)} %fusion.76), channel_id=1, source_target_pairs={{0,1},{1,2},{2,3},{3,4},{4,5},{5,6},{6,7},{8,9},{9,10},{10,11},{11... | collective-permute-start | bytes 786440 | tf_op jit(solution)/shard_map/ppermute | solution.py:13
  13.5 2.2 %copy-start = (bf16[2,1024,1024]{2,1,0:T(8,128)(2,1)S(1)}, bf16[2,1024,1024]{2,1,0:T(8,128)(2,1)}, u32[]{:S(2)}) copy-start(bf16[2,1024,1024]{2,1,0:T(8,128)(2,1)} %param.8) | copy-start | bytes 12582916
  16.5 7.8 %collective-permute-start.3 = (f32[64,1,1024]{2,0,1:T(8,128)S(1)}, f32[64,1,1024]{2,0,1:T(8,128)S(1)}, u32[]{:S(2)}, u32[]{:S(2)}) collective-permute-start(f32[64,1,1024]{2,0,1:T(8,128)S(1)} %fusion.79), channel_id=1, source_target_pairs={{0,1},{1,2},{2,3},{3,4},{4,5},{5,6},{6,7},{8,9},{9,10},{10,11},{11... | collective-permute-start | bytes 786440 | tf_op jit(solution)/shard_map/ppermute | solution.py:13
  21.1 3.2 %collective-permute-start.2 = (bf16[64,1,1024]{2,0,1:T(8,128)(2,1)S(1)}, bf16[64,1,1024]{2,0,1:T(8,128)(2,1)S(1)}, u32[]{:S(2)}, u32[]{:S(2)}) collective-permute-start(bf16[64,1,1024]{2,0,1:T(8,128)(2,1)S(1)} %get-tuple-element.24), channel_id=1, source_target_pairs={{1,0},{2,1},{3,2},{4,3},{5,4},{6,5},{7,6},{9,8},{10,9},{11,10},{12... | collective-permute-start | bytes 393224 | tf_op jit(solution)/shard_map/ppermute | solution.py:13
  27.2 8.7 %collective-permute-start.5 = (f32[64,1,1024]{2,0,1:T(8,128)S(1)}, f32[64,1,1024]{2,0,1:T(8,128)S(1)}, u32[]{:S(2)}, u32[]{:S(2)}) collective-permute-start(f32[64,1,1024]{2,0,1:T(8,128)S(1)} %fusion.82), channel_id=1, source_target_pairs={{0,1},{1,2},{2,3},{3,4},{4,5},{5,6},{6,7},{8,9},{9,10},{10,11},{11... | collective-permute-start | bytes 786440 | tf_op jit(solution)/shard_map/ppermute | solution.py:13
  32.7 3.2 %collective-permute-start.4 = (bf16[64,1,1024]{2,0,1:T(8,128)(2,1)S(1)}, bf16[64,1,1024]{2,0,1:T(8,128)(2,1)S(1)}, u32[]{:S(2)}, u32[]{:S(2)}) collective-permute-start(bf16[64,1,1024]{2,0,1:T(8,128)(2,1)S(1)} %get-tuple-element.22), channel_id=1, source_target_pairs={{1,0},{2,1},{3,2},{4,3},{5,4},{6,5},{7,6},{9,8},{10,9},{11,10},{12... | collective-permute-start | bytes 393224 | tf_op jit(solution)/shard_map/ppermute | solution.py:13
  38.7 8.2 %collective-permute-start.7 = (f32[64,1,1024]{2,0,1:T(8,128)S(1)}, f32[64,1,1024]{2,0,1:T(8,128)S(1)}, u32[]{:S(2)}, u32[]{:S(2)}) collective-permute-start(f32[64,1,1024]{2,0,1:T(8,128)S(1)} %fusion.85), channel_id=1, source_target_pairs={{0,1},{1,2},{2,3},{3,4},{4,5},{5,6},{6,7},{8,9},{9,10},{10,11},{11... | collective-permute-start | bytes 786440 | tf_op jit(solution)/shard_map/ppermute | solution.py:13
  43.7 3.2 %collective-permute-start.6 = (bf16[64,1,1024]{2,0,1:T(8,128)(2,1)S(1)}, bf16[64,1,1024]{2,0,1:T(8,128)(2,1)S(1)}, u32[]{:S(2)}, u32[]{:S(2)}) collective-permute-start(bf16[64,1,1024]{2,0,1:T(8,128)(2,1)S(1)} %get-tuple-element.20), channel_id=1, source_target_pairs={{1,0},{2,1},{3,2},{4,3},{5,4},{6,5},{7,6},{9,8},{10,9},{11,10},{12... | collective-permute-start | bytes 393224 | tf_op jit(solution)/shard_map/ppermute | solution.py:13
  90.0 3.2 %copy-start.1 = (bf16[2,1024,1024]{2,1,0:T(8,128)(2,1)S(1)}, bf16[2,1024,1024]{2,1,0:T(8,128)(2,1)}, u32[]{:S(2)}) copy-start(bf16[2,1024,1024]{2,1,0:T(8,128)(2,1)} %param.8) | copy-start | bytes 12582916
  90.7 6.0 %copy-start.3 = (bf16[2,1024,1024]{2,1,0:T(8,128)(2,1)S(1)}, bf16[2,1024,1024]{2,1,0:T(8,128)(2,1)}, u32[]{:S(2)}) copy-start(bf16[2,1024,1024]{2,1,0:T(8,128)(2,1)} %param.9) | copy-start | bytes 12582916
  94.0 4.6 %collective-permute-start.9 = (f32[64,1,1024]{2,0,1:T(8,128)S(1)}, f32[64,1,1024]{2,0,1:T(8,128)S(1)}, u32[]{:S(2)}, u32[]{:S(2)}) collective-permute-start(f32[64,1,1024]{2,0,1:T(8,128)S(1)} %fusion.88), channel_id=1, source_target_pairs={{0,1},{1,2},{2,3},{3,4},{4,5},{5,6},{6,7},{8,9},{9,10},{10,11},{11... | collective-permute-start | bytes 786440 | tf_op jit(solution)/shard_map/ppermute | solution.py:13
  95.4 3.2 %collective-permute-start.8 = (bf16[64,1,1024]{2,0,1:T(8,128)(2,1)S(1)}, bf16[64,1,1024]{2,0,1:T(8,128)(2,1)S(1)}, u32[]{:S(2)}, u32[]{:S(2)}) collective-permute-start(bf16[64,1,1024]{2,0,1:T(8,128)(2,1)S(1)} %get-tuple-element.18), channel_id=1, source_target_pairs={{1,0},{2,1},{3,2},{4,3},{5,4},{6,5},{7,6},{9,8},{10,9},{11,10},{12... | collective-permute-start | bytes 393224 | tf_op jit(solution)/shard_map/ppermute | solution.py:13
  101.4 6.9 %collective-permute-start.11 = (f32[64,1,1024]{2,0,1:T(8,128)S(1)}, f32[64,1,1024]{2,0,1:T(8,128)S(1)}, u32[]{:S(2)}, u32[]{:S(2)}) collective-permute-start(f32[64,1,1024]{2,0,1:T(8,128)S(1)} %fusion.91), channel_id=1, source_target_pairs={{0,1},{1,2},{2,3},{3,4},{4,5},{5,6},{6,7},{8,9},{9,10},{10,11},{11... | collective-permute-start | bytes 786440 | tf_op jit(solution)/shard_map/ppermute | solution.py:13
  105.1 3.2 %collective-permute-start.10 = (bf16[64,1,1024]{2,0,1:T(8,128)(2,1)S(1)}, bf16[64,1,1024]{2,0,1:T(8,128)(2,1)S(1)}, u32[]{:S(2)}, u32[]{:S(2)}) collective-permute-start(bf16[64,1,1024]{2,0,1:T(8,128)(2,1)S(1)} %get-tuple-element.16), channel_id=1, source_target_pairs={{1,0},{2,1},{3,2},{4,3},{5,4},{6,5},{7,6},{9,8},{10,9},{11,10},{12... | collective-permute-start | bytes 393224 | tf_op jit(solution)/shard_map/ppermute | solution.py:13
  111.1 8.2 %collective-permute-start.13 = (f32[64,1,1024]{2,0,1:T(8,128)S(1)}, f32[64,1,1024]{2,0,1:T(8,128)S(1)}, u32[]{:S(2)}, u32[]{:S(2)}) collective-permute-start(f32[64,1,1024]{2,0,1:T(8,128)S(1)} %fusion.94), channel_id=1, source_target_pairs={{0,1},{1,2},{2,3},{3,4},{4,5},{5,6},{6,7},{8,9},{9,10},{10,11},{11... | collective-permute-start | bytes 786440 | tf_op jit(solution)/shard_map/ppermute | solution.py:13
  116.1 3.2 %collective-permute-start.12 = (bf16[64,1,1024]{2,0,1:T(8,128)(2,1)S(1)}, bf16[64,1,1024]{2,0,1:T(8,128)(2,1)S(1)}, u32[]{:S(2)}, u32[]{:S(2)}) collective-permute-start(bf16[64,1,1024]{2,0,1:T(8,128)(2,1)S(1)} %get-tuple-element.14), channel_id=1, source_target_pairs={{1,0},{2,1},{3,2},{4,3},{5,4},{6,5},{7,6},{9,8},{10,9},{11,10},{12... | collective-permute-start | bytes 393224 | tf_op jit(solution)/shard_map/ppermute | solution.py:13
  122.1 8.2 %collective-permute-start.15 = (f32[64,1,1024]{2,0,1:T(8,128)S(1)}, f32[64,1,1024]{2,0,1:T(8,128)S(1)}, u32[]{:S(2)}, u32[]{:S(2)}) collective-permute-start(f32[64,1,1024]{2,0,1:T(8,128)S(1)} %fusion.97), channel_id=1, source_target_pairs={{0,1},{1,2},{2,3},{3,4},{4,5},{5,6},{6,7},{8,9},{9,10},{10,11},{11... | collective-permute-start | bytes 786440 | tf_op jit(solution)/shard_map/ppermute | solution.py:13
  127.1 3.2 %collective-permute-start.14 = (bf16[64,1,1024]{2,0,1:T(8,128)(2,1)S(1)}, bf16[64,1,1024]{2,0,1:T(8,128)(2,1)S(1)}, u32[]{:S(2)}, u32[]{:S(2)}) collective-permute-start(bf16[64,1,1024]{2,0,1:T(8,128)(2,1)S(1)} %get-tuple-element.12), channel_id=1, source_target_pairs={{1,0},{2,1},{3,2},{4,3},{5,4},{6,5},{7,6},{9,8},{10,9},{11,10},{12... | collective-permute-start | bytes 393224 | tf_op jit(solution)/shard_map/ppermute | solution.py:13
  174.1 5.3 %collective-permute-start.16 = (bf16[16,2048]{1,0:T(8,128)(2,1)S(1)}, bf16[16,2048]{1,0:T(8,128)(2,1)S(1)}, u32[]{:S(2)}, u32[]{:S(2)}) collective-permute-start(bf16[16,2048]{1,0:T(8,128)(2,1)S(1)} %get-tuple-element.9), channel_id=1, source_target_pairs={{0,8},{8,16},{16,24},{1,9},{9,17},{17,25},{2,10},{10,18},{18,26},{... | collective-permute-start | bytes 196616 | tf_op jit(solution)/shard_map/ppermute | solution.py:13
  177.5 6.2 %collective-permute-start.17 = (bf16[16,2048]{1,0:T(8,128)(2,1)S(1)}, bf16[16,2048]{1,0:T(8,128)(2,1)S(1)}, u32[]{:S(2)}, u32[]{:S(2)}) collective-permute-start(bf16[16,2048]{1,0:T(8,128)(2,1)S(1)} %get-tuple-element.10), channel_id=1, source_target_pairs={{8,0},{16,8},{24,16},{9,1},{17,9},{25,17},{10,2},{18,10},{26,18},{... | collective-permute-start | bytes 196616 | tf_op jit(solution)/shard_map/ppermute | solution.py:13
where the time goes:
time: 212 us
  blocking collectives  83.7 us (39%)
  starting transfers between devices  48.5 us (23%)
  matrix products  34.9 us (16%)
  other arithmetic  24.2 us (11%)
  waiting for transfers between devices  14.7 us (7%)
  local copies, waits for them, and re-layouts  3.69 us (2%)
    psum x2, blocking collectives, orthonormal(): gram = lax.psum(inner_products(flat, flat), 'layer') / length_all  57.7 us
    ppermute x18, starting transfers between devices, shifted(): return lax.ppermute(block, axis, route)  48.5 us
    psum x1, blocking collectives, per_device(): lax.psum((inner_products(below_high, low_edge), inner_products(above_low,...  26 us
    ppermute x18, waiting for transfers between devices, shifted(): return lax.ppermute(block, axis, route)  14.7 us
    another operation x6, other arithmetic, orthonormal(): return left_solve(jnp.linalg.cholesky(gram), flat)  13.1 us
    dot_general x8, matrix products, apply_operator(): jnp.einsum('kle,lde->kld', following, couplings, preferred_element_type=j...  11.6 us
    another operation x4, other arithmetic, left_solve(): lax.linalg.triangular_solve(factor, right_side, left_side=True, lower=True)  11.1 us
    dot_general x8, matrix products, apply_operator(): jnp.einsum('kld,lde->kle', rounded, diag_blocks, preferred_element_type=j...  8.95 us
  transfers between devices with their start and end apart: 18, of which 9 were waited for; matrix products, arithmetic and copies ran while one was open for 5% of the time, Pallas kernels for 0%

commit v1 on v0

v1 whole, which is shorter than its diff:
```python
import functools

import jax
import jax.numpy as jnp
from jax import lax
from jax.experimental import pallas as pl
from jax.experimental.pallas import tpu as pltpu
from jax.sharding import PartitionSpec as P

EDGE = 16
DEG = 4
HIGHEST = lax.Precision.HIGHEST


def shifted(block, axis, distance):
    devices = range(lax.axis_size(axis))
    route = [(i - distance, i) for i in devices if i - distance in devices]
    return lax.ppermute(block, axis, route)


def swapped(block, axis, first):
    route = []
    for i in range(first, lax.axis_size(axis) - 1, 2):
        route += [(i, i + 1), (i + 1, i)]
    return lax.ppermute(block, axis, route)


def summed(block, axis):
    size = lax.axis_size(axis)
    if size & (size - 1) or size == 1:
        return lax.psum(block, axis)
    block = block + swapped(block, axis, 0)
    if size <= 8:
        others = [
            lax.ppermute(block, axis, [(i, i ^ step) for i in range(size)])
            for step in range(2, size, 2)
        ]
        for other in others:
            block = block + other
        return block
    step = 2
    while step < size:
        block = block + lax.ppermute(block, axis, [(i, i ^ step) for i in range(size)])
        step *= 2
    return block


def inner_products(first, second):
    return jnp.einsum("kn,jn->kj", first, second, precision=HIGHEST)


def inverse_factor(gram):
    size = gram.shape[0]
    row = lax.broadcasted_iota(jnp.int32, (size, size), 0)
    column = lax.broadcasted_iota(jnp.int32, (size, size), 1)
    work = jnp.concatenate([gram, jnp.where(row == column, 1.0, 0.0)], 1)
    below = lax.broadcasted_iota(jnp.int32, (size, 1), 0)
    pivots = jnp.zeros((size, 1), jnp.float32)
    for j in range(size):
        pivot_row = work[j : j + 1]
        pivot = pivot_row[:, j : j + 1]
        factor = jnp.where(below > j, work[:, j : j + 1] / pivot, 0.0)
        pivots = jnp.where(below == j, pivot, pivots)
        work = work - factor * pivot_row
    return lax.rsqrt(pivots) * work[:, size:]


def factor_kernel(gram_ref, inverse_ref):
    inverse_ref[...] = inverse_factor(gram_ref[...])


def final_kernel(edge, gram_ref, below_gram_ref, above_gram_ref, below_cross_ref, above_cross_ref, out_ref):
    dot = functools.partial(jnp.dot, precision=HIGHEST, preferred_element_type=jnp.float32)
    size = gram_ref.shape[0]
    own = inverse_factor(gram_ref[...])
    below = inverse_factor(below_gram_ref[...])[size - edge :]
    above = inverse_factor(above_gram_ref[...])
    low_t = dot(dot(own[:edge, :edge], below_cross_ref[...].T), below.T)
    high_t = dot(dot(own[size - edge :], above_cross_ref[...].T), above.T)
    out_ref[:, :size] = own
    out_ref[:, size:] = jnp.zeros((size, size + edge), jnp.float32)
    out_ref[:edge, size : 2 * size] = -dot(low_t, below)
    out_ref[size - edge :, 2 * size :] = -dot(high_t, above)


def per_device(vectors, diag_blocks, couplings, bounds):
    count_vec, layers, width = vectors.shape[1:]
    length_all = lax.axis_size("layer") * layers * width
    bottom = bounds[0, 0].astype(jnp.float32) / 64.0
    summit = bounds[0, 1].astype(jnp.float32) / 64.0
    centre = (bottom + summit) / 2.0
    half_width = (summit - bottom) / 2.0
    even = lax.axis_index("layer") % 2 == 0

    def product(block, matrix):
        return jnp.dot(block, matrix, preferred_element_type=jnp.float32)

    def product_t(block, matrix):
        return lax.dot_general(
            block, matrix, (((1,), (1,)), ((), ())), preferred_element_type=jnp.float32
        )

    def apply_operator(now):
        rounded = [block.astype(jnp.bfloat16) for block in now]
        tail = product(rounded[-1], couplings[layers - 1]).astype(jnp.bfloat16)
        outer = swapped(jnp.where(even, rounded[0], tail), "layer", 1)
        inner = swapped(jnp.where(even, tail, rounded[0]), "layer", 0)
        result = [product(rounded[l], diag_blocks[l]) for l in range(layers)]
        for l in range(layers - 1):
            result[l] = result[l] + product_t(rounded[l + 1], couplings[l])
            result[l + 1] = result[l + 1] + product(rounded[l], couplings[l])
        result[0] = result[0] + jnp.where(even, outer, inner).astype(jnp.float32)
        following = jnp.where(even, inner, outer)
        result[-1] = result[-1] + product_t(following, couplings[layers - 1])
        return result

    def filter_block(start):
        previous = start
        image = apply_operator(start)
        current = [(image[l] - centre * start[l]) / half_width for l in range(layers)]
        for degree_index in range(DEG - 1):
            image = apply_operator(current)
            following = [
                2.0 * (image[l] - centre * current[l]) / half_width - previous[l]
                for l in range(layers)
            ]
            previous = current
            current = following
        return current

    def gram_of(blocks):
        return sum(inner_products(block, block) for block in blocks)

    current = filter_block([vectors[0, :, l] for l in range(layers)])
    gram = summed(gram_of(current), "layer") / length_all
    inverse = pl.pallas_call(
        factor_kernel, out_shape=jax.ShapeDtypeStruct(gram.shape, jnp.float32)
    )(gram)
    current = [jnp.dot(inverse, block, precision=HIGHEST) for block in current]
    current = filter_block(current)

    flat = jnp.concatenate(current, 1)
    rounded = flat.astype(jnp.bfloat16)
    below = shifted(rounded, "cuts", 1)
    above = shifted(rounded[:EDGE], "cuts", -1)
    own_gram = inner_products(flat, flat)
    below_wide = below.astype(jnp.float32)
    above_wide = above.astype(jnp.float32)
    parts = [
        own_gram,
        product_t(below, below),
        inner_products(flat, above_wide),
        inner_products(below_wide, flat[:EDGE]),
        jnp.pad(product_t(above, above), ((0, count_vec - EDGE), (0, 0))),
    ]
    total = summed(jnp.concatenate(parts, 1), "layer") / length_all
    slice_at = lax.axis_index("cuts")
    gram = total[:, :count_vec]
    below_gram = jnp.where(slice_at > 0, total[:, count_vec : 2 * count_vec], jnp.eye(count_vec))
    rest = total[:, 2 * count_vec :]
    above_gram = jnp.where(
        slice_at < lax.axis_size("cuts") - 1, rest[:EDGE, 2 * EDGE :], jnp.eye(EDGE)
    )
    weights = pl.pallas_call(
        functools.partial(final_kernel, EDGE),
        out_shape=jax.ShapeDtypeStruct((count_vec, 2 * count_vec + EDGE), jnp.float32),
    )(gram, below_gram, above_gram, rest[:, EDGE : 2 * EDGE], rest[:, :EDGE].T)
    stacked = jnp.concatenate([flat, below_wide, above_wide], 0)
    result = jnp.dot(weights, stacked, precision=HIGHEST)
    return result.reshape(1, count_vec, layers, width)


def solution(mesh):
    in_specs = (
        P("cuts", None, "layer", None),
        P("layer", None, None),
        P("layer", None, None),
        P("cuts", None),
    )
    out_specs = P("cuts", None, "layer", None)
    return jax.shard_map(
        per_device, mesh=mesh, in_specs=in_specs, out_specs=out_specs, check_vma=False
    )
```

time: 212 us -> 148 us (0.70)
  blocking collectives: 83.7 us -> 0 us
  other arithmetic: 24.2 us -> 1.07 us
  Pallas kernels: 0 us -> 15.7 us
  starting transfers between devices: 48.5 us -> 58.3 us
  matrix products: 34.9 us -> 42.6 us
  waiting for transfers between devices: 14.7 us -> 19.7 us
  local copies, waits for them, and re-layouts: 3.69 us -> 7.63 us
    psum x3 -> x0, blocking collectives: 83.7 us -> none  [the longest x2 57.7 us: orthonormal(): gram = lax.psum(inner_products(flat, flat), 'layer') / length_all]
    ppermute x0 -> x24, starting transfers between devices: none -> 53.6 us  [the longest x18 41.9 us: swapped(): return lax.ppermute(block, axis, route)]
    ppermute x18 -> x2, starting transfers between devices: 48.5 us -> 4.7 us  [shifted(): return lax.ppermute(block, axis, route)]
    another operation x10 -> x0, other arithmetic: 24.1 us -> none  [the longest x6 13.1 us: orthonormal(): return left_solve(jnp.linalg.cholesky(gram), flat)]
    pallas_call x0 -> x2, Pallas kernels: none -> 15.7 us  [the longest x1 8.65 us: per_device(): pl.pallas_call(functools.partial(final_kernel, EDGE), out_shape=jax.Shape...]
    ppermute x0 -> x24, waiting for transfers between devices: none -> 15 us  [the longest x6 11.9 us: summed(): lax.ppermute(block, axis, [(i, i ^ step) for i in range(size)])]
    ppermute x18 -> x2, waiting for transfers between devices: 14.7 us -> 4.62 us  [shifted(): return lax.ppermute(block, axis, route)]
    dot_general x38 -> x58, matrix products: 33.7 us -> 42.6 us  [the longest x32 22.5 us: product(): return jnp.dot(block, matrix, preferred_element_type=jnp.float32)]
  transfers between devices with their start and end apart: 18 -> 26, of which waited for: 9 -> 11; matrix products, arithmetic and copies ran while one was open for 5% -> 7% of each run, Pallas kernels for 0% -> 0%
where the time goes in v1:
time: 148 us; the launch traced here: 147 us
  starting transfers between devices  58.3 us (39%)
  matrix products  42.6 us (29%)
  waiting for transfers between devices  19.7 us (13%)
  Pallas kernels  15.7 us (11%)
  local copies, waits for them, and re-layouts  7.63 us (5%)
  between operations  1.93 us (1%)
    ppermute x18, starting transfers between devices, swapped(): return lax.ppermute(block, axis, route)  41.9 us
    dot_general x32, matrix products, product(): return jnp.dot(block, matrix, preferred_element_type=jnp.float32)  22.5 us
    dot_general x18, matrix products, product_t(): lax.dot_general(block, matrix, (((1,), (1,)), ((), ())), preferred_elemen...  14.4 us
    ppermute x6, waiting for transfers between devices, summed(): lax.ppermute(block, axis, [(i, i ^ step) for i in range(size)])  11.9 us
    ppermute x6, starting transfers between devices, summed(): lax.ppermute(block, axis, [(i, i ^ step) for i in range(size)])  11.7 us
    pallas_call x1, Pallas kernels, per_device(): pl.pallas_call(functools.partial(final_kernel, EDGE), out_shape=jax.Shape...  8.65 us
    pallas_call x1, Pallas kernels, per_device(): pl.pallas_call(factor_kernel, out_shape=jax.ShapeDtypeStruct(gram.shape,...  7.05 us
    ppermute x2, starting transfers between devices, shifted(): return lax.ppermute(block, axis, route)  4.7 us
  transfers between devices with their start and end apart: 26, of which 11 were waited for; matrix products, arithmetic and copies ran while one was open for 7% of the time, Pallas kernels for 0%

profile of v1, /device:TPU:0, one launch (start us, length us, event | category | flops | bytes accessed | tf_op | source)
XLA Modules:
  0.0 146.9 jit_solution(5412248377111335899)
XLA Ops:
  0.0 1.7 %fusion.389 = (f32[1,64,1,1024]{3,2,1,0:T(1,128)S(1)}, f32[1,64,1,1024]{3,2,1,0:T(1,128)S(1)}) fusion(f32[1,64,2,1024]{3,2,1,0:T(2,128)} %param.4), kind=kLoop, calls=%fused_computation.303 | loop fusion | bytes 1048576 | tf_op jit(solution)/shard_map/slice | solution.py:134
  1.7 2.2 %broadcast_select_fusion.15 = (bf16[64,1024]{1,0:T(8,128)(2,1)S(1)}, bf16[64,1024]{1,0:T(8,128)(2,1)S(1)}) fusion(pred[]{:T(512)S(6)} %eq.11, f32[1,64,1,1024]{3,2,1,0:T(1,128)S(1)} %get-tuple-element.24, bf16[2,1024,1024]{2,1,0:T(8,128)(2,1)} %param.6, f32[1,64,1,1024]{3,2,1,0:T(1,128)S(1)} %get-tuple-element.25), kind=kOutput, calls=%fused_computation.237 | convolution fusion | flops 134414336 | bytes 2883585 | tf_op jit(solution)/shard_map/dot_general | solution.py:96
  3.9 0.7 collective-permute-start
  4.6 4.4 %collective-permute-start.1 = (bf16[64,1024]{1,0:T(8,128)(2,1)S(1)}, bf16[64,1024]{1,0:T(8,128)(2,1)S(1)}, u32[]{:S(2)}, u32[]{:S(2)}) collective-permute-start(bf16[64,1024]{1,0:T(8,128)(2,1)S(1)} %get-tuple-element.27), channel_id=1, source_target_pairs={{0,1},{1,0},{2,3},{3,2},{4,5},{5,4},{6,7},{7,6},{8,9},{9,8},{10,11... | collective-permute-start | bytes 393224 | tf_op jit(solution)/shard_map/ppermute | solution.py:25
  9.0 2.1 %fusion.14 = f32[64,1024]{1,0:T(8,128)S(1)} fusion(bf16[2,1024,1024]{2,1,0:T(8,128)(2,1)} %param.5, f32[1,64,1,1024]{3,2,1,0:T(1,128)S(1)} %get-tuple-element.25), kind=kOutput, calls=%fused_computation.14 | convolution fusion | flops 134217728 | bytes 2621440 | tf_op jit(solution)/shard_map/dot_general | solution.py:96
  11.6 0.8 fusion.78
  12.4 0.6 fusion.390
  14.2 0.8 fusion.158
  15.5 0.8 fusion.74
  17.8 0.7 collective-permute-start.2
  18.5 3.0 %collective-permute-start.3 = (bf16[64,1024]{1,0:T(8,128)(2,1)S(1)}, bf16[64,1024]{1,0:T(8,128)(2,1)S(1)}, u32[]{:S(2)}, u32[]{:S(2)}) collective-permute-start(bf16[64,1024]{1,0:T(8,128)(2,1)S(1)} %get-tuple-element.22), channel_id=1, source_target_pairs={{0,1},{1,0},{2,3},{3,2},{4,5},{5,4},{6,7},{7,6},{8,9},{9,8},{10,11... | collective-permute-start | bytes 393224 | tf_op jit(solution)/shard_map/ppermute | solution.py:25
  22.5 0.8 fusion.242
  24.4 0.7 collective-permute-start.4
  25.5 4.6 %collective-permute-start.5 = (bf16[64,1024]{1,0:T(8,128)(2,1)S(1)}, bf16[64,1024]{1,0:T(8,128)(2,1)S(1)}, u32[]{:S(2)}, u32[]{:S(2)}) collective-permute-start(bf16[64,1024]{1,0:T(8,128)(2,1)S(1)} %get-tuple-element.19), channel_id=1, source_target_pairs={{0,1},{1,0},{2,3},{3,2},{4,5},{5,4},{6,7},{7,6},{8,9},{9,8},{10,11... | collective-permute-start | bytes 393224 | tf_op jit(solution)/shard_map/ppermute | solution.py:25
  30.2 0.8 fusion.70
  31.2 0.8 fusion.245
  32.9 0.8 fusion.66
  34.8 0.8 collective-permute-start.6
  35.6 4.1 %collective-permute-start.7 = (bf16[64,1024]{1,0:T(8,128)(2,1)S(1)}, bf16[64,1024]{1,0:T(8,128)(2,1)S(1)}, u32[]{:S(2)}, u32[]{:S(2)}) collective-permute-start(bf16[64,1024]{1,0:T(8,128)(2,1)S(1)} %get-tuple-element.16), channel_id=1, source_target_pairs={{0,1},{1,0},{2,3},{3,2},{4,5},{5,4},{6,7},{7,6},{8,9},{9,8},{10,11... | collective-permute-start | bytes 393224 | tf_op jit(solution)/shard_map/ppermute | solution.py:25
  41.2 0.8 fusion.248
  42.4 1.5 %collective-permute-start.8 = (f32[64,64]{1,0:T(8,128)S(1)}, f32[64,64]{1,0:T(8,128)S(1)}, u32[]{:S(2)}, u32[]{:S(2)}) collective-permute-start(f32[64,64]{1,0:T(8,128)S(1)} %convolution_add_fusion), channel_id=1, source_target_pairs={{0,1},{1,0},{2,3},{3,2},{4,5},{5,4},{6,7},{7,6},{8,9},{9,8},{10,11... | collective-permute-start | bytes 49160 | tf_op jit(solution)/shard_map/ppermute | solution.py:25
  43.9 0.9 collective-permute-done.8
  44.8 2.9 %collective-permute-start.10 = (f32[64,64]{1,0:T(8,128)S(1)}, f32[64,64]{1,0:T(8,128)S(1)}, u32[]{:S(2)}, u32[]{:S(2)}) collective-permute-start(f32[64,64]{1,0:T(8,128)S(1)} %add.152), channel_id=1, source_target_pairs={{0,4},{1,5},{2,6},{3,7},{4,0},{5,1},{6,2},{7,3},{8,12},{9,13},{10,... | collective-permute-start | bytes 49160 | tf_op jit(solution)/shard_map/ppermute | solution.py:35
  47.7 1.3 collective-permute-start.11
  49.6 3.8 %collective-permute-done.11 = f32[64,64]{1,0:T(8,128)S(1)} collective-permute-done((f32[64,64]{1,0:T(8,128)S(1)}, f32[64,64]{1,0:T(8,128)S(1)}, u32[]{:S(2)}, u32[]{:S(2)}) %collective-permute-start.11) | collective-permute-done | bytes 16416 | tf_op jit(solution)/shard_map/ppermute | solution.py:35
  53.4 0.6 add_multiply_fusion.1.gram_ref
  54.0 7.1 %shard_map.46 = f32[64,64]{1,0:T(8,128)} custom-call(f32[64,64]{1,0:T(8,128)} %add_multiply_fusion.1.gram_ref), custom_call_target="tpu_custom_call" | custom-call | tf_op jit(solution)/shard_map/pallas_call | solution.py:136
  61.1 1.1 fusion.392
  62.2 1.1 fusion.393
  63.3 2.5 %fusion.62 = f32[64,1024]{1,0:T(8,128)S(1)} fusion(f32[64,1024]{1,0:T(8,128)S(1)} %fusion.393, bf16[2,1024,1024]{2,1,0:T(8,128)(2,1)} %param.6), kind=kOutput, calls=%fused_computation.62 | convolution fusion | flops 134283264 | bytes 2621440 | tf_op jit(solution)/shard_map/dot_general | solution.py:99
  65.8 2.1 %fusion.6 = f32[64,1024]{1,0:T(8,128)S(1)} fusion(bf16[2,1024,1024]{2,1,0:T(8,128)(2,1)} %param.5, f32[64,1024]{1,0:T(8,128)S(1)} %fusion.393), kind=kOutput, calls=%fused_computation.6 | convolution fusion | flops 134283264 | bytes 2621440 | tf_op jit(solution)/shard_map/dot_general | solution.py:96
  68.4 2.1 %fusion.116 = f32[64,1024]{1,0:T(8,128)S(1)} fusion(f32[64,1024]{1,0:T(8,128)S(1)} %fusion.62, bf16[64,1024]{1,0:T(8,128)(2,1)S(1)} %get-tuple-element.15, bf16[2,1024,1024]{2,1,0:T(8,128)(2,1)} %param.5), kind=kOutput, calls=%fused_computation.108 | convolution fusion | flops 134283264 | bytes 2752512 | tf_op jit(solution)/shard_map/dot_general | solution.py:96
  70.6 0.7 collective-permute-start.12
  72.0 0.8 fusion.194
  72.7 0.8 copy-done.3
  74.5 4.7 %collective-permute-start.15 = (bf16[64,1024]{1,0:T(8,128)(2,1)S(1)}, bf16[64,1024]{1,0:T(8,128)(2,1)S(1)}, u32[]{:S(2)}, u32[]{:S(2)}) collective-permute-start(bf16[64,1024]{1,0:T(8,128)(2,1)S(1)} %broadcast_select_fusion.4), channel_id=1, source_target_pairs={{0,1},{1,0},{2,3},{3,2},{4,5},{5,4},{6,7},{7,6},{8,9},{9,8},{10,11... | collective-permute-start | bytes 393224 | tf_op jit(solution)/shard_map/ppermute | solution.py:25
  79.7 0.7 collective-permute-start.14
  80.4 0.8 fusion.58
  81.2 0.8 fusion.251
  83.6 4.9 %collective-permute-start.17 = (bf16[64,1024]{1,0:T(8,128)(2,1)S(1)}, bf16[64,1024]{1,0:T(8,128)(2,1)S(1)}, u32[]{:S(2)}, u32[]{:S(2)}) collective-permute-start(bf16[64,1024]{1,0:T(8,128)(2,1)S(1)} %broadcast_select_fusion.2), channel_id=1, source_target_pairs={{0,1},{1,0},{2,3},{3,2},{4,5},{5,4},{6,7},{7,6},{8,9},{9,8},{10,11... | collective-permute-start | bytes 393224 | tf_op jit(solution)/shard_map/ppermute | solution.py:25
  89.0 0.9 collective-permute-start.16
  89.9 0.8 fusion.54
  90.7 0.8 fusion.254
  91.9 0.8 fusion.50
  94.3 4.7 %collective-permute-start.19 = (bf16[64,1024]{1,0:T(8,128)(2,1)S(1)}, bf16[64,1024]{1,0:T(8,128)(2,1)S(1)}, u32[]{:S(2)}, u32[]{:S(2)}) collective-permute-start(bf16[64,1024]{1,0:T(8,128)(2,1)S(1)} %broadcast_select_fusion), channel_id=1, source_target_pairs={{0,1},{1,0},{2,3},{3,2},{4,5},{5,4},{6,7},{7,6},{8,9},{9,8},{10,11... | collective-permute-start | bytes 393224 | tf_op jit(solution)/shard_map/ppermute | solution.py:25
  99.0 0.7 collective-permute-start.18
  100.2 0.8 fusion.257
  101.1 3.4 %collective-permute-start.20 = (bf16[64,2048]{1,0:T(8,128)(2,1)S(1)}, bf16[64,2048]{1,0:T(8,128)(2,1)S(1)}, u32[]{:S(2)}, u32[]{:S(2)}) collective-permute-start(bf16[64,2048]{1,0:T(8,128)(2,1)S(1)} %fusion.300), channel_id=1, source_target_pairs={{0,8},{8,16},{16,24},{1,9},{9,17},{17,25},{2,10},{10,18},{18,26},{... | collective-permute-start | bytes 786440 | tf_op jit(solution)/shard_map/ppermute | solution.py:18
  104.5 1.3 collective-permute-start.21
  106.4 4.6 %collective-permute-done.21 = bf16[16,2048]{1,0:T(8,128)(2,1)S(1)} collective-permute-done((bf16[16,2048]{1,0:T(8,128)(2,1)S(1)}, bf16[16,2048]{1,0:T(8,128)(2,1)S(1)}, u32[]{:S(2)}, u32[]{:S(2)}) %collective-permute-start.21) | collective-permute-done | bytes 65568 | tf_op jit(solution)/shard_map/ppermute | solution.py:18
  112.1 4.0 %collective-permute-start.22 = (f32[64,176]{0,1:T(8,128)S(1)}, f32[64,176]{0,1:T(8,128)S(1)}, u32[]{:S(2)}, u32[]{:S(2)}) collective-permute-start(f32[64,176]{0,1:T(8,128)S(1)} %constant_dynamic-update-slice_fusion), channel_id=1, source_target_pairs={{0,1},{1,0},{2,3},{3,2},{4,5},{5,4},{6,7},{7,6},{8,9},{9,8},{10,11... | collective-permute-start | bytes 135176 | tf_op jit(solution)/shard_map/ppermute | solution.py:25
  116.1 0.9 collective-permute-done.22
  117.0 5.0 %collective-permute-start.23 = (f32[64,176]{0,1:T(8,128)S(1)}, f32[64,176]{0,1:T(8,128)S(1)}, u32[]{:S(2)}, u32[]{:S(2)}) collective-permute-start(f32[64,176]{0,1:T(8,128)S(1)} %add.172), channel_id=1, source_target_pairs={{0,2},{1,3},{2,0},{3,1},{4,6},{5,7},{6,4},{7,5},{8,10},{9,11},{10,... | collective-permute-start | bytes 135176 | tf_op jit(solution)/shard_map/ppermute | solution.py:35
  122.0 0.7 collective-permute-start.24
  122.7 1.7 %collective-permute-start.25 = (f32[64,176]{0,1:T(8,128)S(1)}, f32[64,176]{0,1:T(8,128)S(1)}, u32[]{:S(2)}, u32[]{:S(2)}) collective-permute-start(f32[64,176]{0,1:T(8,128)S(1)} %add.172), channel_id=1, source_target_pairs={{0,6},{1,7},{2,4},{3,5},{4,2},{5,3},{6,0},{7,1},{8,14},{9,15},{10,... | collective-permute-start | bytes 135176 | tf_op jit(solution)/shard_map/ppermute | solution.py:35
  125.0 7.0 %collective-permute-done.24 = f32[64,176]{0,1:T(8,128)S(1)} collective-permute-done((f32[64,176]{0,1:T(8,128)S(1)}, f32[64,176]{0,1:T(8,128)S(1)}, u32[]{:S(2)}, u32[]{:S(2)}) %collective-permute-start.24) | collective-permute-done | bytes 45088 | tf_op jit(solution)/shard_map/ppermute | solution.py:35
  132.1 0.6 slice_bitcast_fusion
  132.7 0.7 copy.10.below_gram_ref
  133.4 0.7 copy.9.gram_ref
  134.1 0.7 copy.12.below_cross_ref
  134.8 0.7 copy.11.above_gram_ref
  135.4 8.6 %shard_map.47 = f32[64,144]{1,0:T(8,128)} custom-call(f32[64,64]{1,0:T(8,128)} %copy.9.gram_ref, f32[64,64]{1,0:T(8,128)} %copy.10.below_gram_ref, f32[16,16]{1,0:T(8,128)} %copy.11.above_gram_ref, f32[64,16]{1,0:T(8,128)} %copy.12.below_cross_ref, f32[16,64]{1,0:T(8,128)} %get-tuple-element.28.above_cross_ref), custom_call_target="tpu_custom_call" | custom-call | tf_op jit(solution)/shard_map/pallas_call | solution.py:164
  144.1 1.6 %fusion.96 = f32[64,2048]{1,0:T(8,128)S(1)} fusion(f32[64,144]{1,0:T(8,128)} %shard_map.47, f32[16,2048]{1,0:T(8,128)S(1)} %convert_element_type.173, f32[64,2048]{1,0:T(8,128)S(1)} %convert_element_type.172, f32[64,1024]{1,0:T(8,128)S(1)} %fusion.257, f32[64,1024]{1,0:T(8,128)S(1)} %divide_subtract_fusion), kind=kOutput, calls=%fused_computation.96 | convolution fusion | flops 227377152 | bytes 1740800 | tf_op jit(solution)/shard_map/dot_general | solution.py:169
  145.7 1.2 reshape.20
  (86 shorter events, 19.3 us)
Async XLA Ops:
  1.7 9.4 %copy-start = (bf16[2,1024,1024]{2,1,0:T(8,128)(2,1)S(1)}, bf16[2,1024,1024]{2,1,0:T(8,128)(2,1)}, u32[]{:S(2)}) copy-start(bf16[2,1024,1024]{2,1,0:T(8,128)(2,1)} %param.6) | copy-start | bytes 12582916
  3.9 10.3 %collective-permute-start = (bf16[64,1024]{1,0:T(8,128)(2,1)S(1)}, bf16[64,1024]{1,0:T(8,128)(2,1)S(1)}, u32[]{:S(2)}, u32[]{:S(2)}) collective-permute-start(bf16[64,1024]{1,0:T(8,128)(2,1)S(1)} %get-tuple-element.26), channel_id=1, source_target_pairs={{1,2},{2,1},{3,4},{4,3},{5,6},{6,5},{9,10},{10,9},{11,12},{12,11},... | collective-permute-start | bytes 393224 | tf_op jit(solution)/shard_map/ppermute | solution.py:25
  4.6 9.7 %collective-permute-start.1 = (bf16[64,1024]{1,0:T(8,128)(2,1)S(1)}, bf16[64,1024]{1,0:T(8,128)(2,1)S(1)}, u32[]{:S(2)}, u32[]{:S(2)}) collective-permute-start(bf16[64,1024]{1,0:T(8,128)(2,1)S(1)} %get-tuple-element.27), channel_id=1, source_target_pairs={{0,1},{1,0},{2,3},{3,2},{4,5},{5,4},{6,7},{7,6},{8,9},{9,8},{10,11... | collective-permute-start | bytes 393224 | tf_op jit(solution)/shard_map/ppermute | solution.py:25
  11.1 1.3 copy-start.4
  11.6 3.4 %copy-start.2 = (bf16[2,1024,1024]{2,1,0:T(8,128)(2,1)S(1)}, bf16[2,1024,1024]{2,1,0:T(8,128)(2,1)}, u32[]{:S(2)}) copy-start(bf16[2,1024,1024]{2,1,0:T(8,128)(2,1)} %param.5) | copy-start | bytes 12582916
  17.8 4.2 %collective-permute-start.2 = (bf16[64,1024]{1,0:T(8,128)(2,1)S(1)}, bf16[64,1024]{1,0:T(8,128)(2,1)S(1)}, u32[]{:S(2)}, u32[]{:S(2)}) collective-permute-start(bf16[64,1024]{1,0:T(8,128)(2,1)S(1)} %broadcast_select_fusion.13), channel_id=1, source_target_pairs={{1,2},{2,1},{3,4},{4,3},{5,6},{6,5},{9,10},{10,9},{11,12},{12,11},... | collective-permute-start | bytes 393224 | tf_op jit(solution)/shard_map/ppermute | solution.py:25
  18.5 4.0 %collective-permute-start.3 = (bf16[64,1024]{1,0:T(8,128)(2,1)S(1)}, bf16[64,1024]{1,0:T(8,128)(2,1)S(1)}, u32[]{:S(2)}, u32[]{:S(2)}) collective-permute-start(bf16[64,1024]{1,0:T(8,128)(2,1)S(1)} %get-tuple-element.22), channel_id=1, source_target_pairs={{0,1},{1,0},{2,3},{3,2},{4,5},{5,4},{6,7},{7,6},{8,9},{9,8},{10,11... | collective-permute-start | bytes 393224 | tf_op jit(solution)/shard_map/ppermute | solution.py:25
  24.4 6.6 %collective-permute-start.4 = (bf16[64,1024]{1,0:T(8,128)(2,1)S(1)}, bf16[64,1024]{1,0:T(8,128)(2,1)S(1)}, u32[]{:S(2)}, u32[]{:S(2)}) collective-permute-start(bf16[64,1024]{1,0:T(8,128)(2,1)S(1)} %broadcast_select_fusion.11), channel_id=1, source_target_pairs={{1,2},{2,1},{3,4},{4,3},{5,6},{6,5},{9,10},{10,9},{11,12},{12,11},... | collective-permute-start | bytes 393224 | tf_op jit(solution)/shard_map/ppermute | solution.py:25
  25.5 5.6 %collective-permute-start.5 = (bf16[64,1024]{1,0:T(8,128)(2,1)S(1)}, bf16[64,1024]{1,0:T(8,128)(2,1)S(1)}, u32[]{:S(2)}, u32[]{:S(2)}) collective-permute-start(bf16[64,1024]{1,0:T(8,128)(2,1)S(1)} %get-tuple-element.19), channel_id=1, source_target_pairs={{0,1},{1,0},{2,3},{3,2},{4,5},{5,4},{6,7},{7,6},{8,9},{9,8},{10,11... | collective-permute-start | bytes 393224 | tf_op jit(solution)/shard_map/ppermute | solution.py:25
  34.8 5.5 %collective-permute-start.6 = (bf16[64,1024]{1,0:T(8,128)(2,1)S(1)}, bf16[64,1024]{1,0:T(8,128)(2,1)S(1)}, u32[]{:S(2)}, u32[]{:S(2)}) collective-permute-start(bf16[64,1024]{1,0:T(8,128)(2,1)S(1)} %broadcast_select_fusion.9), channel_id=1, source_target_pairs={{1,2},{2,1},{3,4},{4,3},{5,6},{6,5},{9,10},{10,9},{11,12},{12,11},... | collective-permute-start | bytes 393224 | tf_op jit(solution)/shard_map/ppermute | solution.py:25
  35.6 5.1 %collective-permute-start.7 = (bf16[64,1024]{1,0:T(8,128)(2,1)S(1)}, bf16[64,1024]{1,0:T(8,128)(2,1)S(1)}, u32[]{:S(2)}, u32[]{:S(2)}) collective-permute-start(bf16[64,1024]{1,0:T(8,128)(2,1)S(1)} %get-tuple-element.16), channel_id=1, source_target_pairs={{0,1},{1,0},{2,3},{3,2},{4,5},{5,4},{6,7},{7,6},{8,9},{9,8},{10,11... | collective-permute-start | bytes 393224 | tf_op jit(solution)/shard_map/ppermute | solution.py:25
  42.4 2.4 %collective-permute-start.8 = (f32[64,64]{1,0:T(8,128)S(1)}, f32[64,64]{1,0:T(8,128)S(1)}, u32[]{:S(2)}, u32[]{:S(2)}) collective-permute-start(f32[64,64]{1,0:T(8,128)S(1)} %convolution_add_fusion), channel_id=1, source_target_pairs={{0,1},{1,0},{2,3},{3,2},{4,5},{5,4},{6,7},{7,6},{8,9},{9,8},{10,11... | collective-permute-start | bytes 49160 | tf_op jit(solution)/shard_map/ppermute | solution.py:25
  44.8 4.8 %collective-permute-start.10 = (f32[64,64]{1,0:T(8,128)S(1)}, f32[64,64]{1,0:T(8,128)S(1)}, u32[]{:S(2)}, u32[]{:S(2)}) collective-permute-start(f32[64,64]{1,0:T(8,128)S(1)} %add.152), channel_id=1, source_target_pairs={{0,4},{1,5},{2,6},{3,7},{4,0},{5,1},{6,2},{7,3},{8,12},{9,13},{10,... | collective-permute-start | bytes 49160 | tf_op jit(solution)/shard_map/ppermute | solution.py:35
  47.7 5.7 %collective-permute-start.11 = (f32[64,64]{1,0:T(8,128)S(1)}, f32[64,64]{1,0:T(8,128)S(1)}, u32[]{:S(2)}, u32[]{:S(2)}) collective-permute-start(f32[64,64]{1,0:T(8,128)S(1)} %add.152), channel_id=1, source_target_pairs={{0,6},{1,7},{2,4},{3,5},{4,2},{5,3},{6,0},{7,1},{8,14},{9,15},{10,... | collective-permute-start | bytes 49160 | tf_op jit(solution)/shard_map/ppermute | solution.py:35
  49.0 4.4 %collective-permute-start.9 = (f32[64,64]{1,0:T(8,128)S(1)}, f32[64,64]{1,0:T(8,128)S(1)}, u32[]{:S(2)}, u32[]{:S(2)}) collective-permute-start(f32[64,64]{1,0:T(8,128)S(1)} %add.152), channel_id=1, source_target_pairs={{0,2},{1,3},{2,0},{3,1},{4,6},{5,7},{6,4},{7,5},{8,10},{9,11},{10,... | collective-permute-start | bytes 49160 | tf_op jit(solution)/shard_map/ppermute | solution.py:35
  63.3 4.6 %copy-start.1 = (bf16[2,1024,1024]{2,1,0:T(8,128)(2,1)S(1)}, bf16[2,1024,1024]{2,1,0:T(8,128)(2,1)}, u32[]{:S(2)}) copy-start(bf16[2,1024,1024]{2,1,0:T(8,128)(2,1)} %param.6) | copy-start | bytes 12582916
  70.5 1.4 collective-permute-start.13
  70.6 1.3 collective-permute-start.12
  71.3 2.2 %copy-start.3 = (bf16[2,1024,1024]{2,1,0:T(8,128)(2,1)S(1)}, bf16[2,1024,1024]{2,1,0:T(8,128)(2,1)}, u32[]{:S(2)}) copy-start(bf16[2,1024,1024]{2,1,0:T(8,128)(2,1)} %param.5) | copy-start | bytes 12582916
  74.5 6.7 %collective-permute-start.15 = (bf16[64,1024]{1,0:T(8,128)(2,1)S(1)}, bf16[64,1024]{1,0:T(8,128)(2,1)S(1)}, u32[]{:S(2)}, u32[]{:S(2)}) collective-permute-start(bf16[64,1024]{1,0:T(8,128)(2,1)S(1)} %broadcast_select_fusion.4), channel_id=1, source_target_pairs={{0,1},{1,0},{2,3},{3,2},{4,5},{5,4},{6,7},{7,6},{8,9},{9,8},{10,11... | collective-permute-start | bytes 393224 | tf_op jit(solution)/shard_map/ppermute | solution.py:25
  79.7 1.4 collective-permute-start.14
  83.6 7.1 %collective-permute-start.17 = (bf16[64,1024]{1,0:T(8,128)(2,1)S(1)}, bf16[64,1024]{1,0:T(8,128)(2,1)S(1)}, u32[]{:S(2)}, u32[]{:S(2)}) collective-permute-start(bf16[64,1024]{1,0:T(8,128)(2,1)S(1)} %broadcast_select_fusion.2), channel_id=1, source_target_pairs={{0,1},{1,0},{2,3},{3,2},{4,5},{5,4},{6,7},{7,6},{8,9},{9,8},{10,11... | collective-permute-start | bytes 393224 | tf_op jit(solution)/shard_map/ppermute | solution.py:25
  89.0 1.7 %collective-permute-start.16 = (bf16[64,1024]{1,0:T(8,128)(2,1)S(1)}, bf16[64,1024]{1,0:T(8,128)(2,1)S(1)}, u32[]{:S(2)}, u32[]{:S(2)}) collective-permute-start(bf16[64,1024]{1,0:T(8,128)(2,1)S(1)} %get-tuple-element.8), channel_id=1, source_target_pairs={{1,2},{2,1},{3,4},{4,3},{5,6},{6,5},{9,10},{10,9},{11,12},{12,11},... | collective-permute-start | bytes 393224 | tf_op jit(solution)/shard_map/ppermute | solution.py:25
  94.3 5.9 %collective-permute-start.19 = (bf16[64,1024]{1,0:T(8,128)(2,1)S(1)}, bf16[64,1024]{1,0:T(8,128)(2,1)S(1)}, u32[]{:S(2)}, u32[]{:S(2)}) collective-permute-start(bf16[64,1024]{1,0:T(8,128)(2,1)S(1)} %broadcast_select_fusion), channel_id=1, source_target_pairs={{0,1},{1,0},{2,3},{3,2},{4,5},{5,4},{6,7},{7,6},{8,9},{9,8},{10,11... | collective-permute-start | bytes 393224 | tf_op jit(solution)/shard_map/ppermute | solution.py:25
  99.0 1.2 collective-permute-start.18
  101.1 10.1 %collective-permute-start.20 = (bf16[64,2048]{1,0:T(8,128)(2,1)S(1)}, bf16[64,2048]{1,0:T(8,128)(2,1)S(1)}, u32[]{:S(2)}, u32[]{:S(2)}) collective-permute-start(bf16[64,2048]{1,0:T(8,128)(2,1)S(1)} %fusion.300), channel_id=1, source_target_pairs={{0,8},{8,16},{16,24},{1,9},{9,17},{17,25},{2,10},{10,18},{18,26},{... | collective-permute-start | bytes 786440 | tf_op jit(solution)/shard_map/ppermute | solution.py:18
  104.5 6.5 %collective-permute-start.21 = (bf16[16,2048]{1,0:T(8,128)(2,1)S(1)}, bf16[16,2048]{1,0:T(8,128)(2,1)S(1)}, u32[]{:S(2)}, u32[]{:S(2)}) collective-permute-start(bf16[16,2048]{1,0:T(8,128)(2,1)S(1)} %slice.48), channel_id=1, source_target_pairs={{8,0},{16,8},{24,16},{9,1},{17,9},{25,17},{10,2},{18,10},{26,18},{... | collective-permute-start | bytes 196616 | tf_op jit(solution)/shard_map/ppermute | solution.py:18
  112.1 5.0 %collective-permute-start.22 = (f32[64,176]{0,1:T(8,128)S(1)}, f32[64,176]{0,1:T(8,128)S(1)}, u32[]{:S(2)}, u32[]{:S(2)}) collective-permute-start(f32[64,176]{0,1:T(8,128)S(1)} %constant_dynamic-update-slice_fusion), channel_id=1, source_target_pairs={{0,1},{1,0},{2,3},{3,2},{4,5},{5,4},{6,7},{7,6},{8,9},{9,8},{10,11... | collective-permute-start | bytes 135176 | tf_op jit(solution)/shard_map/ppermute | solution.py:25
  117.0 8.0 %collective-permute-start.23 = (f32[64,176]{0,1:T(8,128)S(1)}, f32[64,176]{0,1:T(8,128)S(1)}, u32[]{:S(2)}, u32[]{:S(2)}) collective-permute-start(f32[64,176]{0,1:T(8,128)S(1)} %add.172), channel_id=1, source_target_pairs={{0,2},{1,3},{2,0},{3,1},{4,6},{5,7},{6,4},{7,5},{8,10},{9,11},{10,... | collective-permute-start | bytes 135176 | tf_op jit(solution)/shard_map/ppermute | solution.py:35
  122.0 10.0 %collective-permute-start.24 = (f32[64,176]{0,1:T(8,128)S(1)}, f32[64,176]{0,1:T(8,128)S(1)}, u32[]{:S(2)}, u32[]{:S(2)}) collective-permute-start(f32[64,176]{0,1:T(8,128)S(1)} %add.172), channel_id=1, source_target_pairs={{0,4},{1,5},{2,6},{3,7},{4,0},{5,1},{6,2},{7,3},{8,12},{9,13},{10,... | collective-permute-start | bytes 135176 | tf_op jit(solution)/shard_map/ppermute | solution.py:35
  122.7 9.3 %collective-permute-start.25 = (f32[64,176]{0,1:T(8,128)S(1)}, f32[64,176]{0,1:T(8,128)S(1)}, u32[]{:S(2)}, u32[]{:S(2)}) collective-permute-start(f32[64,176]{0,1:T(8,128)S(1)} %add.172), channel_id=1, source_target_pairs={{0,6},{1,7},{2,4},{3,5},{4,2},{5,3},{6,0},{7,1},{8,14},{9,15},{10,... | collective-permute-start | bytes 135176 | tf_op jit(solution)/shard_map/ppermute | solution.py:35

commit v2 on v0

v2 whole, which is shorter than its diff:
```python
import functools

import jax
import jax.numpy as jnp
from jax import lax
from jax.experimental import pallas as pl
from jax.experimental.pallas import tpu as pltpu
from jax.sharding import PartitionSpec as P

EDGE = 16
DEG = 4
ROWS = 8
HIGHEST = lax.Precision.HIGHEST
BF16 = jnp.bfloat16
F32 = jnp.float32
VMEM = pl.BlockSpec(memory_space=pltpu.VMEM)
SMEM = pl.BlockSpec(memory_space=pltpu.SMEM)


def exchanged(block, first):
    count, slices = lax.axis_size("layer"), lax.axis_size("cuts")
    route = []
    for cut in range(slices):
        for i in range(count):
            j = i + 1 if (i - first) % 2 == 0 else i - 1
            to = (cut, j) if 0 <= j < count else (cut ^ 1 if cut ^ 1 < slices else cut, i)
            route.append((cut * count + i, to[0] * count + to[1]))
    return lax.ppermute(block, ("cuts", "layer"), route)


def rotated(block, distance):
    size = lax.axis_size("cuts")
    return lax.ppermute(block, "cuts", [(i, (i + distance) % size) for i in range(size)])


def partial_sums(block):
    size = lax.axis_size("layer")
    if size & (size - 1) or size == 1:
        return [lax.psum(block, "layer")]
    block = block + lax.ppermute(block, "layer", [(i, i ^ 1) for i in range(size)])
    reach = 2
    while size // reach > 4:
        block = block + lax.ppermute(block, "layer", [(i, i ^ reach) for i in range(size)])
        reach *= 2
    return [block] + [
        lax.ppermute(block, "layer", [(i, i ^ step) for i in range(size)])
        for step in range(reach, size, reach)
    ]


def product(block, matrix):
    return jnp.dot(block, matrix, preferred_element_type=F32)


def product_t(block, matrix, precision=None):
    return lax.dot_general(
        block, matrix, (((1,), (1,)), ((), ())), precision=precision, preferred_element_type=F32
    )


def exact(first, second):
    return jnp.dot(first, second, precision=HIGHEST, preferred_element_type=F32)


def inverse_factor(gram):
    size = gram.shape[0]
    row = lax.broadcasted_iota(jnp.int32, (size, size), 0)
    column = lax.broadcasted_iota(jnp.int32, (size, size), 1)
    work = jnp.concatenate([jnp.where(row == column, 1.0, 0.0), gram], 1)
    finished = []
    for start in range(0, size, ROWS):
        left = size - start
        at = lax.broadcasted_iota(jnp.int32, (left, 2 * size), 0)
        lines = [
            jnp.broadcast_to(work[:, size + start + c : size + start + c + 1], (left, 2 * size))
            for c in range(ROWS)
        ]
        pivots = jnp.zeros((ROWS, 2 * size), F32)
        for c in range(ROWS):
            pivot = lines[c][c : c + 1]
            factor = jnp.where(at > c, lines[c] * (1.0 / pivot), 0.0)
            pivots = jnp.where(at[:ROWS] == c, pivot, pivots)
            work = work - factor * work[c : c + 1]
            for d in range(c + 1, ROWS):
                lines[d] = lines[d] - factor * lines[d][c : c + 1]
        finished.append(lax.rsqrt(pivots) * work[:ROWS])
        work = work[ROWS:]
    return jnp.concatenate(finished, 0)[:, :size]


def send(at, rounded_ref, coupling, inner_ref, outer_ref):
    last = rounded_ref.shape[0] - 1
    tail = product(rounded_ref[last], coupling).astype(BF16)
    first = rounded_ref[0]

    @pl.when(at % 2 == 0)
    def _():
        inner_ref[...] = tail
        outer_ref[...] = first

    @pl.when(at % 2 == 1)
    def _():
        inner_ref[...] = first
        outer_ref[...] = tail


def enter_kernel(at_ref, vectors_ref, couplings_ref, start_ref, rounded_ref, inner_ref, outer_ref):
    layers = start_ref.shape[0]
    for l in range(layers):
        block = vectors_ref[:, l, :]
        start_ref[l] = block
        rounded_ref[l] = block.astype(BF16)
    send(at_ref[0], rounded_ref, couplings_ref[layers - 1], inner_ref, outer_ref)


def interior_kernel(at_ref, rounded_ref, arrived_ref, diag_ref, couplings_ref, sum_ref):
    layers = rounded_ref.shape[0]
    for l in range(layers):
        term = product(rounded_ref[l], diag_ref[l])
        if l > 0:
            term = term + product(rounded_ref[l - 1], couplings_ref[l - 1])
        if l < layers - 1:
            term = term + product_t(rounded_ref[l + 1], couplings_ref[l])
        sum_ref[l] = term

    @pl.when(at_ref[0] % 2 == 0)
    def _():
        sum_ref[layers - 1] += product_t(arrived_ref[...], couplings_ref[layers - 1])

    @pl.when(at_ref[0] % 2 == 1)
    def _():
        sum_ref[0] += arrived_ref[...].astype(F32)


def advance(count, first_step, at, shift_ref, sum_ref, arrived_ref, couplings_ref, now_ref, before_ref, next_ref):
    layers = sum_ref.shape[0]

    @pl.when((at % 2 == 0) & (at > 0))
    def _():
        sum_ref[0] += arrived_ref[...].astype(F32)

    @pl.when((at % 2 == 1) & (at < count - 1))
    def _():
        sum_ref[layers - 1] += product_t(arrived_ref[...], couplings_ref[layers - 1])

    centre, scale = shift_ref[0], shift_ref[1]
    for l in range(layers):
        block = (sum_ref[l] - centre * now_ref[l]) * scale
        if not first_step:
            block = 2.0 * block - before_ref[l]
        next_ref[l] = block


def step_kernel(
    count, first_step, at_ref, shift_ref, sum_in_ref, arrived_ref, couplings_ref, now_ref, before_ref,
    next_ref, rounded_ref, inner_ref, outer_ref, sum_ref,
):
    at = at_ref[0]
    sum_ref[...] = sum_in_ref[...]
    advance(
        count, first_step, at, shift_ref, sum_ref, arrived_ref, couplings_ref, now_ref, before_ref, next_ref
    )
    rounded_ref[...] = next_ref[...].astype(BF16)
    send(at, rounded_ref, couplings_ref[sum_ref.shape[0] - 1], inner_ref, outer_ref)


def last_kernel(
    count, at_ref, shift_ref, sum_in_ref, arrived_ref, couplings_ref, now_ref, before_ref,
    next_ref, rounded_ref, gram_ref, sum_ref,
):
    sum_ref[...] = sum_in_ref[...]
    advance(
        count, False, at_ref[0], shift_ref, sum_ref, arrived_ref, couplings_ref, now_ref, before_ref, next_ref
    )
    rounded_ref[...] = next_ref[...].astype(BF16)
    gram_ref[...] = sum(
        product_t(next_ref[l], next_ref[l], HIGHEST) for l in range(next_ref.shape[0])
    )


def normal_kernel(parts, length, at_ref, *refs):
    grams, (filtered_ref, couplings_ref, start_ref, rounded_ref, inner_ref, outer_ref) = refs[:parts], refs[parts:]
    gram = sum(ref[...] for ref in grams) * (1.0 / length)
    inverse = inverse_factor(gram)
    layers = start_ref.shape[0]
    for l in range(layers):
        block = exact(inverse, filtered_ref[l])
        start_ref[l] = block
        rounded_ref[l] = block.astype(BF16)
    send(at_ref[0], rounded_ref, couplings_ref[layers - 1], inner_ref, outer_ref)


def cross_kernel(gram_ref, rounded_ref, below_ref, above_ref, out_ref):
    size, edge = gram_ref.shape[0], above_ref.shape[1]
    layers = range(rounded_ref.shape[0])
    out_ref[:, :size] = gram_ref[...]
    out_ref[:, size : 2 * size] = sum(product_t(below_ref[l], below_ref[l]) for l in layers)
    out_ref[:, 2 * size : 2 * size + edge] = sum(
        product_t(below_ref[l], rounded_ref[l, :edge]) for l in layers
    )
    out_ref[:, 2 * size + edge : 2 * size + 2 * edge] = sum(
        product_t(rounded_ref[l], above_ref[l]) for l in layers
    )
    out_ref[:edge, 2 * size + 2 * edge :] = sum(
        product_t(above_ref[l], above_ref[l]) for l in layers
    )
    out_ref[edge:, 2 * size + 2 * edge :] = jnp.zeros((size - edge, edge), F32)


def final_kernel(parts, length, slices, cut_ref, *refs):
    grams, (filtered_ref, below_ref, above_ref, out_ref) = refs[:parts], refs[parts:]
    layers, size, _ = filtered_ref.shape
    edge = above_ref.shape[1]
    total = sum(ref[...] for ref in grams) * (1.0 / length)

    def identity(extent):
        row = lax.broadcasted_iota(jnp.int32, (extent, extent), 0)
        column = lax.broadcasted_iota(jnp.int32, (extent, extent), 1)
        return jnp.where(row == column, 1.0, 0.0)

    has_below = (cut_ref[0] > 0).astype(F32)
    has_above = (cut_ref[0] < slices - 1).astype(F32)
    below_gram = total[:, size : 2 * size] * has_below + identity(size) * (1.0 - has_below)
    above_gram = total[:edge, 2 * size + 2 * edge :] * has_above + identity(edge) * (1.0 - has_above)
    below_cross = total[:, 2 * size : 2 * size + edge] * has_below
    above_cross = total[:, 2 * size + edge : 2 * size + 2 * edge] * has_above
    own = inverse_factor(total[:, :size])
    below = inverse_factor(below_gram)[size - edge :]
    above = inverse_factor(above_gram)
    low_t = exact(own[:edge, :edge], product_t(below_cross.T, below, HIGHEST))
    high_t = exact(own[size - edge :], product_t(above_cross, above, HIGHEST))
    low_weights = exact(low_t, below)
    high_weights = exact(high_t, above)
    for l in range(layers):
        block = exact(own, filtered_ref[l])
        out_ref[:edge, l, :] = block[:edge] - exact(low_weights, below_ref[l].astype(F32))
        out_ref[edge : size - edge, l, :] = block[edge : size - edge]
        out_ref[size - edge :, l, :] = block[size - edge :] - exact(
            high_weights, above_ref[l].astype(F32)
        )


def per_device(vectors, diag_blocks, couplings, bounds):
    vectors = vectors[0]
    count_vec, layers, width = vectors.shape
    count = lax.axis_size("layer")
    length_all = count * layers * width
    low = bounds[0, 0].astype(F32) / 64.0
    high = bounds[0, 1].astype(F32) / 64.0
    shift = jnp.stack([(low + high) / 2.0, 2.0 / (high - low)])
    at = lax.axis_index("layer").astype(jnp.int32).reshape(1)
    cut = lax.axis_index("cuts").astype(jnp.int32).reshape(1)

    field = (layers, count_vec, width)
    field32 = jax.ShapeDtypeStruct(field, F32)
    field16 = jax.ShapeDtypeStruct(field, BF16)
    message = jax.ShapeDtypeStruct((count_vec, width), BF16)
    gram_type = jax.ShapeDtypeStruct((count_vec, count_vec), F32)
    scratch = [pltpu.VMEM(field, F32)]

    def call(kernel, outs, scalars, *operands, scratch_shapes=(), flops=0):
        moved = sum(x.size * x.dtype.itemsize for x in operands)
        return pl.pallas_call(
            kernel,
            out_shape=outs,
            in_specs=[SMEM] * len(scalars) + [VMEM] * len(operands),
            out_specs=jax.tree.map(lambda _: VMEM, outs),
            scratch_shapes=list(scratch_shapes),
            compiler_params=pltpu.CompilerParams(vmem_limit_bytes=32 * 2**20),
            cost_estimate=pl.CostEstimate(flops=flops, bytes_accessed=moved, transcendentals=0),
        )(*scalars, *operands)

    one = 2 * count_vec * width * width

    def filter_block(start, rounded, inner, outer):
        before, now = start, start
        for step in range(DEG):
            outer_in = exchanged(outer, 1)
            inner_in = exchanged(inner, 0)
            partial = call(
                interior_kernel, field32, [at], rounded, inner_in, diag_blocks, couplings,
                flops=(3 * layers - 1) * one,
            )
            operands = (partial, outer_in, couplings, now, before)
            if step < DEG - 1:
                following, rounded, inner, outer = call(
                    functools.partial(step_kernel, count, step == 0),
                    (field32, field16, message, message), [at, shift], *operands,
                    scratch_shapes=scratch, flops=2 * one,
                )
                before, now = now, following
            else:
                return call(
                    functools.partial(last_kernel, count),
                    (field32, field16, gram_type), [at, shift], *operands,
                    scratch_shapes=scratch, flops=2 * one,
                )

    outs = (field32, field16, message, message)
    start = call(enter_kernel, outs, [at], vectors, couplings, flops=one)
    filtered, rounded, gram = filter_block(*start)
    grams = partial_sums(gram)
    start = call(
        functools.partial(normal_kernel, len(grams), length_all), outs, [at], *grams, filtered, couplings,
        flops=2 * one,
    )
    filtered, rounded, gram = filter_block(*start)
    below = rotated(rounded, 1)
    above = rotated(rounded[:, :EDGE], -1)
    cross = call(
        cross_kernel, jax.ShapeDtypeStruct((count_vec, 2 * count_vec + 3 * EDGE), F32), [],
        gram, rounded, below, above,
    )
    grams = partial_sums(cross)
    result = call(
        functools.partial(final_kernel, len(grams), length_all, lax.axis_size("cuts")),
        jax.ShapeDtypeStruct((count_vec, layers, width), F32), [cut], *grams, filtered, below, above,
    )
    return result[None]


def solution(mesh):
    in_specs = (
        P("cuts", None, "layer", None),
        P("layer", None, None),
        P("layer", None, None),
        P("cuts", None),
    )
    out_specs = P("cuts", None, "layer", None)
    return jax.shard_map(
        per_device, mesh=mesh, in_specs=in_specs, out_specs=out_specs, check_vma=False
    )
```

time: 212 us -> 102 us (0.48)
  blocking collectives: 83.7 us -> 0 us
  Pallas kernels: 0 us -> 40.9 us
  matrix products: 34.9 us -> 0 us
  other arithmetic: 24.2 us -> 0.09 us
  starting transfers between devices: 48.5 us -> 29 us
  waiting for transfers between devices: 14.7 us -> 23.9 us
  local copies, waits for them, and re-layouts: 3.69 us -> 6.03 us
    psum x3 -> x0, blocking collectives: 83.7 us -> none  [the longest x2 57.7 us: orthonormal(): gram = lax.psum(inner_products(flat, flat), 'layer') / length_all]
    pallas_call x0 -> x20, Pallas kernels: none -> 40.9 us  [call(): pl.pallas_call(kernel, out_shape=outs, in_specs=[SMEM] * len(scalars) + [...]
    dot_general x38 -> x0, matrix products: 33.7 us -> none  [the longest x8 11.6 us: apply_operator(): jnp.einsum('kle,lde->kld', following, couplings, preferred_element_type=j...]
    another operation x10 -> x1, other arithmetic: 24.1 us -> 0.08 us  [per_device(): shift = jnp.stack([(low + high) / 2.0, 2.0 / (high - low)])]
    ppermute x18 -> x26, starting transfers between devices: 48.5 us -> 29 us  [the longest x16 16.6 us: exchanged(): return lax.ppermute(block, ('cuts', 'layer'), route)]
    ppermute x18 -> x26, waiting for transfers between devices: 14.7 us -> 23.9 us  [the longest x2 8.2 us: rotated(): lax.ppermute(block, 'cuts', [(i, (i + distance) % size) for i in range(si...]
    unnamed x13 -> x10, local copies, waits for them, and re-layouts: 1.41 us -> 5.44 us
  transfers between devices with their start and end apart: 18 -> 26, of which waited for: 9 -> 15; matrix products, arithmetic and copies ran while one was open for 5% -> 1% of each run, Pallas kernels for 0% -> 20%
where the time goes in v2:
time: 102 us; the launch traced here: 101 us
  Pallas kernels  40.9 us (40%)
  starting transfers between devices  29 us (28%)
  waiting for transfers between devices  23.9 us (23%)
  local copies, waits for them, and re-layouts  6.03 us (6%)
  between operations  1.48 us (1%)
    pallas_call x20, Pallas kernels, call(): pl.pallas_call(kernel, out_shape=outs, in_specs=[SMEM] * len(scalars) + [...  40.9 us
    ppermute x16, starting transfers between devices, exchanged(): return lax.ppermute(block, ('cuts', 'layer'), route)  16.6 us
    ppermute x6, starting transfers between devices, partial_sums(): lax.ppermute(block, 'layer', [(i, i ^ step) for i in range(size)])  8.83 us
    ppermute x2, waiting for transfers between devices, rotated(): lax.ppermute(block, 'cuts', [(i, (i + distance) % size) for i in range(si...  8.2 us
    ppermute x16, waiting for transfers between devices, exchanged(): return lax.ppermute(block, ('cuts', 'layer'), route)  7.21 us
    ppermute x6, waiting for transfers between devices, partial_sums(): lax.ppermute(block, 'layer', [(i, i ^ step) for i in range(size)])  6.36 us
    unnamed x10, local copies, waits for them, and re-layouts  5.44 us
    ppermute x2, starting transfers between devices, rotated(): lax.ppermute(block, 'cuts', [(i, (i + distance) % size) for i in range(si...  2.98 us
  transfers between devices with their start and end apart: 26, of which 15 were waited for; matrix products, arithmetic and copies ran while one was open for 1% of the time, Pallas kernels for 20%

profile of v2, /device:TPU:0, one launch (start us, length us, event | category | flops | bytes accessed | tf_op | source)
XLA Modules:
  0.0 101.3 jit_solution(6981614109608246130)
XLA Ops:
  0.0 2.2 %copy-done = bf16[2,1024,1024]{2,1,0:T(8,128)(2,1)S(1)} copy-done((bf16[2,1024,1024]{2,1,0:T(8,128)(2,1)S(1)}, bf16[2,1024,1024]{2,1,0:T(8,128)(2,1)}, u32[]{:S(2)}) %copy-start) | copy-done | bytes 4194328
  2.2 1.0 %copy-done.3 = f32[1,64,2,1024]{3,2,1,0:T(2,128)S(1)} copy-done((f32[1,64,2,1024]{3,2,1,0:T(2,128)S(1)}, f32[1,64,2,1024]{3,2,1,0:T(2,128)}, u32[]{:S(2)}) %copy-start.3) | copy-done | bytes 524312
  3.2 1.2 %shard_map.46 = (f32[2,64,1024]{2,1,0:T(8,128)S(1)}, bf16[2,64,1024]{2,1,0:T(8,128)(2,1)S(1)}, bf16[64,1024]{1,0:T(8,128)(2,1)S(1)}, bf16[64,1024]{1,0:T(8,128)(2,1)S(1)}) custom-call(s32[1]{0:T(128)} %bitcast.1.at_ref, f32[64,2,1024]{2,1,0:T(2,128)S(1)} %bitcast.6, bf16[2,1024,1024]{2,1,0:T(8,128)(2,1)S(1)} %copy-done), custom_call_target="tpu_custom_call" | custom-call | flops 134217728 | bytes 4718592 | tf_op jit(solution)/shard_map/pallas_call | solution.py:263
  4.5 0.5 collective-permute-start
  5.0 2.6 %collective-permute-start.1 = (bf16[64,1024]{1,0:T(8,128)(2,1)S(1)}, bf16[64,1024]{1,0:T(8,128)(2,1)S(1)}, u32[]{:S(2)}, u32[]{:S(2)}) collective-permute-start(bf16[64,1024]{1,0:T(8,128)(2,1)S(1)} %get-tuple-element.44), channel_id=1, source_target_pairs={{0,8},{1,2},{2,1},{3,4},{4,3},{5,6},{6,5},{7,15},{8,0},{9,10},{10,... | collective-permute-start | bytes 393224 | tf_op jit(solution)/shard_map/ppermute | solution.py:28
  7.6 0.6 fusion
  9.4 0.1 pad_maximum_fusion.shift_ref
  9.5 2.2 %copy-done.2 = bf16[2,1024,1024]{2,1,0:T(8,128)(2,1)S(1)} copy-done((bf16[2,1024,1024]{2,1,0:T(8,128)(2,1)S(1)}, bf16[2,1024,1024]{2,1,0:T(8,128)(2,1)}, u32[]{:S(2)}) %copy-start.2) | copy-done | bytes 4194328
  11.7 2.6 %shard_map.47.sum_in_ref = f32[2,64,1024]{2,1,0:T(8,128)S(1)} custom-call(s32[1]{0:T(128)} %bitcast.1.at_ref, bf16[2,64,1024]{2,1,0:T(8,128)(2,1)S(1)} %get-tuple-element.42.rounded_ref, bf16[64,1024]{1,0:T(8,128)(2,1)S(1)} %collective-permute-done.arrived_ref, bf16[2,1024,1024]{2,1,0:T(8,128)(2,1)S(1)} %copy-done.2, bf16[2,1024,1024]{2,1,0:T(8,128)(2,1)S(1)} %copy-done.1), custom_call_target="tpu_custom_call" | custom-call | flops 671088640 | bytes 8781824 | tf_op jit(solution)/shard_map/pallas_call | solution.py:263
  14.3 1.1 %shard_map.48 = (f32[2,64,1024]{2,1,0:T(8,128)S(1)}, bf16[2,64,1024]{2,1,0:T(8,128)(2,1)S(1)}, bf16[64,1024]{1,0:T(8,128)(2,1)S(1)}, bf16[64,1024]{1,0:T(8,128)(2,1)S(1)}) custom-call(s32[1]{0:T(128)} %bitcast.1.at_ref, f32[2]{0:T(128)S(1)} %pad_maximum_fusion.shift_ref, f32[2,64,1024]{2,1,0:T(8,128)S(1)} %shard_map.47.sum_in_ref, ...), custom_call_target="tpu_custom_call" | custom-call | flops 268435456 | bytes 5898240 | tf_op jit(solution)/shard_map/pallas_call | solution.py:263
  15.4 0.3 collective-permute-start.2
  15.8 1.5 %collective-permute-start.3 = (bf16[64,1024]{1,0:T(8,128)(2,1)S(1)}, bf16[64,1024]{1,0:T(8,128)(2,1)S(1)}, u32[]{:S(2)}, u32[]{:S(2)}) collective-permute-start(bf16[64,1024]{1,0:T(8,128)(2,1)S(1)} %get-tuple-element.48), channel_id=1, source_target_pairs={{0,8},{1,2},{2,1},{3,4},{4,3},{5,6},{6,5},{7,15},{8,0},{9,10},{10,... | collective-permute-start | bytes 393224 | tf_op jit(solution)/shard_map/ppermute | solution.py:28
  17.2 2.6 %shard_map.49.sum_in_ref = f32[2,64,1024]{2,1,0:T(8,128)S(1)} custom-call(s32[1]{0:T(128)} %bitcast.1.at_ref, bf16[2,64,1024]{2,1,0:T(8,128)(2,1)S(1)} %get-tuple-element.46.rounded_ref, bf16[64,1024]{1,0:T(8,128)(2,1)S(1)} %collective-permute-done.2.arrived_ref, bf16[2,1024,1024]{2,1,0:T(8,128)(2,1)S(1)} %copy-done.2, bf16[2,1024,1024]{2,1,0:T(8,128)(2,1)S(1)} %copy-done.1), custom_call_target="tpu_custom_call" | custom-call | flops 671088640 | bytes 8781824 | tf_op jit(solution)/shard_map/pallas_call | solution.py:263
  19.8 0.9 collective-permute-done.3.arrived_ref
  20.7 1.1 %shard_map.50 = (f32[2,64,1024]{2,1,0:T(8,128)S(1)}, bf16[2,64,1024]{2,1,0:T(8,128)(2,1)S(1)}, bf16[64,1024]{1,0:T(8,128)(2,1)S(1)}, bf16[64,1024]{1,0:T(8,128)(2,1)S(1)}) custom-call(s32[1]{0:T(128)} %bitcast.1.at_ref, f32[2]{0:T(128)S(1)} %pad_maximum_fusion.shift_ref, f32[2,64,1024]{2,1,0:T(8,128)S(1)} %shard_map.49.sum_in_ref, ...), custom_call_target="tpu_custom_call" | custom-call | flops 268435456 | bytes 5898240 | tf_op jit(solution)/shard_map/pallas_call | solution.py:263
  21.9 0.8 collective-permute-start.4
  22.7 1.3 %collective-permute-start.5 = (bf16[64,1024]{1,0:T(8,128)(2,1)S(1)}, bf16[64,1024]{1,0:T(8,128)(2,1)S(1)}, u32[]{:S(2)}, u32[]{:S(2)}) collective-permute-start(bf16[64,1024]{1,0:T(8,128)(2,1)S(1)} %get-tuple-element.52), channel_id=1, source_target_pairs={{0,8},{1,2},{2,1},{3,4},{4,3},{5,6},{6,5},{7,15},{8,0},{9,10},{10,... | collective-permute-start | bytes 393224 | tf_op jit(solution)/shard_map/ppermute | solution.py:28
  24.0 2.6 %shard_map.51.sum_in_ref = f32[2,64,1024]{2,1,0:T(8,128)S(1)} custom-call(s32[1]{0:T(128)} %bitcast.1.at_ref, bf16[2,64,1024]{2,1,0:T(8,128)(2,1)S(1)} %get-tuple-element.50.rounded_ref, bf16[64,1024]{1,0:T(8,128)(2,1)S(1)} %collective-permute-done.4.arrived_ref, bf16[2,1024,1024]{2,1,0:T(8,128)(2,1)S(1)} %copy-done.2, bf16[2,1024,1024]{2,1,0:T(8,128)(2,1)S(1)} %copy-done.1), custom_call_target="tpu_custom_call" | custom-call | flops 671088640 | bytes 8781824 | tf_op jit(solution)/shard_map/pallas_call | solution.py:263
  26.6 1.1 %collective-permute-done.5.arrived_ref = bf16[64,1024]{1,0:T(8,128)(2,1)S(1)} collective-permute-done((bf16[64,1024]{1,0:T(8,128)(2,1)S(1)}, bf16[64,1024]{1,0:T(8,128)(2,1)S(1)}, u32[]{:S(2)}, u32[]{:S(2)}) %collective-permute-start.5) | collective-permute-done | bytes 131104 | tf_op jit(solution)/shard_map/ppermute | solution.py:28
  27.7 1.1 %shard_map.52 = (f32[2,64,1024]{2,1,0:T(8,128)S(1)}, bf16[2,64,1024]{2,1,0:T(8,128)(2,1)S(1)}, bf16[64,1024]{1,0:T(8,128)(2,1)S(1)}, bf16[64,1024]{1,0:T(8,128)(2,1)S(1)}) custom-call(s32[1]{0:T(128)} %bitcast.1.at_ref, f32[2]{0:T(128)S(1)} %pad_maximum_fusion.shift_ref, f32[2,64,1024]{2,1,0:T(8,128)S(1)} %shard_map.51.sum_in_ref, ...), custom_call_target="tpu_custom_call" | custom-call | flops 268435456 | bytes 5898240 | tf_op jit(solution)/shard_map/pallas_call | solution.py:263
  28.8 0.6 collective-permute-start.6
  29.4 1.3 %collective-permute-start.7 = (bf16[64,1024]{1,0:T(8,128)(2,1)S(1)}, bf16[64,1024]{1,0:T(8,128)(2,1)S(1)}, u32[]{:S(2)}, u32[]{:S(2)}) collective-permute-start(bf16[64,1024]{1,0:T(8,128)(2,1)S(1)} %get-tuple-element.56), channel_id=1, source_target_pairs={{0,8},{1,2},{2,1},{3,4},{4,3},{5,6},{6,5},{7,15},{8,0},{9,10},{10,... | collective-permute-start | bytes 393224 | tf_op jit(solution)/shard_map/ppermute | solution.py:28
  30.8 2.6 %shard_map.53.sum_in_ref = f32[2,64,1024]{2,1,0:T(8,128)S(1)} custom-call(s32[1]{0:T(128)} %bitcast.1.at_ref, bf16[2,64,1024]{2,1,0:T(8,128)(2,1)S(1)} %get-tuple-element.54.rounded_ref, bf16[64,1024]{1,0:T(8,128)(2,1)S(1)} %collective-permute-done.6.arrived_ref, bf16[2,1024,1024]{2,1,0:T(8,128)(2,1)S(1)} %copy-done.2, bf16[2,1024,1024]{2,1,0:T(8,128)(2,1)S(1)} %copy-done.1), custom_call_target="tpu_custom_call" | custom-call | flops 671088640 | bytes 8781824 | tf_op jit(solution)/shard_map/pallas_call | solution.py:263
  33.4 1.1 %collective-permute-done.7.arrived_ref = bf16[64,1024]{1,0:T(8,128)(2,1)S(1)} collective-permute-done((bf16[64,1024]{1,0:T(8,128)(2,1)S(1)}, bf16[64,1024]{1,0:T(8,128)(2,1)S(1)}, u32[]{:S(2)}, u32[]{:S(2)}) %collective-permute-start.7) | collective-permute-done | bytes 131104 | tf_op jit(solution)/shard_map/ppermute | solution.py:28
  34.4 1.9 %shard_map.54 = (f32[2,64,1024]{2,1,0:T(8,128)S(1)}, bf16[2,64,1024]{2,1,0:T(8,128)(2,1)}, f32[64,64]{1,0:T(8,128)S(1)}) custom-call(s32[1]{0:T(128)} %bitcast.1.at_ref, f32[2]{0:T(128)S(1)} %pad_maximum_fusion.shift_ref, f32[2,64,1024]{2,1,0:T(8,128)S(1)} %shard_map.53.sum_in_ref, bf16[64,1024]{1,0:T(8,128)(2,1)S(1)} %collective-permute-done.7.arrived_ref, ...), custom_call_target="tpu_custom_call" | custom-call | flops 268435456 | bytes 5898240 | tf_op jit(solution)/shard_map/pallas_call | solution.py:263
  36.3 0.5 collective-permute-start.8
  36.8 0.9 collective-permute-done.8
  37.7 0.6 collective-permute-start.11
  38.2 1.5 %collective-permute-start.10 = (f32[64,64]{1,0:T(8,128)S(1)}, f32[64,64]{1,0:T(8,128)S(1)}, u32[]{:S(2)}, u32[]{:S(2)}) collective-permute-start(f32[64,64]{1,0:T(8,128)S(1)} %add.11.refs_0_), channel_id=1, source_target_pairs={{0,4},{1,5},{2,6},{3,7},{4,0},{5,1},{6,2},{7,3},{8,12},{9,13},{10,... | collective-permute-start | bytes 49160 | tf_op jit(solution)/shard_map/ppermute | solution.py:46
  39.8 2.3 %collective-permute-start.9 = (f32[64,64]{1,0:T(8,128)S(1)}, f32[64,64]{1,0:T(8,128)S(1)}, u32[]{:S(2)}, u32[]{:S(2)}) collective-permute-start(f32[64,64]{1,0:T(8,128)S(1)} %add.11.refs_0_), channel_id=1, source_target_pairs={{0,2},{1,3},{2,0},{3,1},{4,6},{5,7},{6,4},{7,5},{8,10},{9,11},{10,... | collective-permute-start | bytes 49160 | tf_op jit(solution)/shard_map/ppermute | solution.py:46
  42.1 1.7 %collective-permute-done.11.refs_3_ = f32[64,64]{1,0:T(8,128)S(1)} collective-permute-done((f32[64,64]{1,0:T(8,128)S(1)}, f32[64,64]{1,0:T(8,128)S(1)}, u32[]{:S(2)}, u32[]{:S(2)}) %collective-permute-start.11) | collective-permute-done | bytes 16416 | tf_op jit(solution)/shard_map/ppermute | solution.py:46
  43.8 0.1 collective-permute-done.10.refs_2_
  43.9 0.3 collective-permute-done.9.refs_1_
  44.2 2.7 %shard_map.55 = (f32[2,64,1024]{2,1,0:T(8,128)S(1)}, bf16[2,64,1024]{2,1,0:T(8,128)(2,1)S(1)}, bf16[64,1024]{1,0:T(8,128)(2,1)S(1)}, bf16[64,1024]{1,0:T(8,128)(2,1)S(1)}) custom-call(s32[1]{0:T(128)} %bitcast.1.at_ref, f32[64,64]{1,0:T(8,128)S(1)} %add.11.refs_0_, f32[64,64]{1,0:T(8,128)S(1)} %collective-permute-done.9.refs_1_, ...), custom_call_target="tpu_custom_call" | custom-call | flops 268435456 | bytes 4784128 | tf_op jit(solution)/shard_map/pallas_call | solution.py:263
  46.9 0.1 collective-permute-start.12
  47.0 1.4 %collective-permute-start.13 = (bf16[64,1024]{1,0:T(8,128)(2,1)S(1)}, bf16[64,1024]{1,0:T(8,128)(2,1)S(1)}, u32[]{:S(2)}, u32[]{:S(2)}) collective-permute-start(bf16[64,1024]{1,0:T(8,128)(2,1)S(1)} %get-tuple-element.62), channel_id=1, source_target_pairs={{0,8},{1,2},{2,1},{3,4},{4,3},{5,6},{6,5},{7,15},{8,0},{9,10},{10,... | collective-permute-start | bytes 393224 | tf_op jit(solution)/shard_map/ppermute | solution.py:28
  48.3 2.6 %shard_map.56.sum_in_ref = f32[2,64,1024]{2,1,0:T(8,128)S(1)} custom-call(s32[1]{0:T(128)} %bitcast.1.at_ref, bf16[2,64,1024]{2,1,0:T(8,128)(2,1)S(1)} %get-tuple-element.60.rounded_ref, bf16[64,1024]{1,0:T(8,128)(2,1)S(1)} %collective-permute-done.12.arrived_ref, bf16[2,1024,1024]{2,1,0:T(8,128)(2,1)S(1)} %copy-done.2, bf16[2,1024,1024]{2,1,0:T(8,128)(2,1)S(1)} %copy-done.1), custom_call_target="tpu_custom_call" | custom-call | flops 671088640 | bytes 8781824 | tf_op jit(solution)/shard_map/pallas_call | solution.py:263
  50.9 1.1 %collective-permute-done.13.arrived_ref = bf16[64,1024]{1,0:T(8,128)(2,1)S(1)} collective-permute-done((bf16[64,1024]{1,0:T(8,128)(2,1)S(1)}, bf16[64,1024]{1,0:T(8,128)(2,1)S(1)}, u32[]{:S(2)}, u32[]{:S(2)}) %collective-permute-start.13) | collective-permute-done | bytes 131104 | tf_op jit(solution)/shard_map/ppermute | solution.py:28
  52.0 1.1 %shard_map.57 = (f32[2,64,1024]{2,1,0:T(8,128)S(1)}, bf16[2,64,1024]{2,1,0:T(8,128)(2,1)S(1)}, bf16[64,1024]{1,0:T(8,128)(2,1)S(1)}, bf16[64,1024]{1,0:T(8,128)(2,1)S(1)}) custom-call(s32[1]{0:T(128)} %bitcast.1.at_ref, f32[2]{0:T(128)S(1)} %pad_maximum_fusion.shift_ref, f32[2,64,1024]{2,1,0:T(8,128)S(1)} %shard_map.56.sum_in_ref, ...), custom_call_target="tpu_custom_call" | custom-call | flops 268435456 | bytes 5898240 | tf_op jit(solution)/shard_map/pallas_call | solution.py:263
  53.1 0.9 collective-permute-start.14
  54.1 1.3 %collective-permute-start.15 = (bf16[64,1024]{1,0:T(8,128)(2,1)S(1)}, bf16[64,1024]{1,0:T(8,128)(2,1)S(1)}, u32[]{:S(2)}, u32[]{:S(2)}) collective-permute-start(bf16[64,1024]{1,0:T(8,128)(2,1)S(1)} %get-tuple-element.66), channel_id=1, source_target_pairs={{0,8},{1,2},{2,1},{3,4},{4,3},{5,6},{6,5},{7,15},{8,0},{9,10},{10,... | collective-permute-start | bytes 393224 | tf_op jit(solution)/shard_map/ppermute | solution.py:28
  55.4 2.6 %shard_map.58.sum_in_ref = f32[2,64,1024]{2,1,0:T(8,128)S(1)} custom-call(s32[1]{0:T(128)} %bitcast.1.at_ref, bf16[2,64,1024]{2,1,0:T(8,128)(2,1)S(1)} %get-tuple-element.64.rounded_ref, bf16[64,1024]{1,0:T(8,128)(2,1)S(1)} %collective-permute-done.14.arrived_ref, bf16[2,1024,1024]{2,1,0:T(8,128)(2,1)S(1)} %copy-done.2, bf16[2,1024,1024]{2,1,0:T(8,128)(2,1)S(1)} %copy-done.1), custom_call_target="tpu_custom_call" | custom-call | flops 671088640 | bytes 8781824 | tf_op jit(solution)/shard_map/pallas_call | solution.py:263
  58.0 1.0 %collective-permute-done.15.arrived_ref = bf16[64,1024]{1,0:T(8,128)(2,1)S(1)} collective-permute-done((bf16[64,1024]{1,0:T(8,128)(2,1)S(1)}, bf16[64,1024]{1,0:T(8,128)(2,1)S(1)}, u32[]{:S(2)}, u32[]{:S(2)}) %collective-permute-start.15) | collective-permute-done | bytes 131104 | tf_op jit(solution)/shard_map/ppermute | solution.py:28
  59.0 1.2 %shard_map.59 = (f32[2,64,1024]{2,1,0:T(8,128)S(1)}, bf16[2,64,1024]{2,1,0:T(8,128)(2,1)S(1)}, bf16[64,1024]{1,0:T(8,128)(2,1)S(1)}, bf16[64,1024]{1,0:T(8,128)(2,1)S(1)}) custom-call(s32[1]{0:T(128)} %bitcast.1.at_ref, f32[2]{0:T(128)S(1)} %pad_maximum_fusion.shift_ref, f32[2,64,1024]{2,1,0:T(8,128)S(1)} %shard_map.58.sum_in_ref, ...), custom_call_target="tpu_custom_call" | custom-call | flops 268435456 | bytes 5898240 | tf_op jit(solution)/shard_map/pallas_call | solution.py:263
  60.2 0.6 collective-permute-start.16
  60.8 1.3 %collective-permute-start.17 = (bf16[64,1024]{1,0:T(8,128)(2,1)S(1)}, bf16[64,1024]{1,0:T(8,128)(2,1)S(1)}, u32[]{:S(2)}, u32[]{:S(2)}) collective-permute-start(bf16[64,1024]{1,0:T(8,128)(2,1)S(1)} %get-tuple-element.70), channel_id=1, source_target_pairs={{0,8},{1,2},{2,1},{3,4},{4,3},{5,6},{6,5},{7,15},{8,0},{9,10},{10,... | collective-permute-start | bytes 393224 | tf_op jit(solution)/shard_map/ppermute | solution.py:28
  62.2 2.6 %shard_map.60.sum_in_ref = f32[2,64,1024]{2,1,0:T(8,128)S(1)} custom-call(s32[1]{0:T(128)} %bitcast.1.at_ref, bf16[2,64,1024]{2,1,0:T(8,128)(2,1)S(1)} %get-tuple-element.68.rounded_ref, bf16[64,1024]{1,0:T(8,128)(2,1)S(1)} %collective-permute-done.16.arrived_ref, bf16[2,1024,1024]{2,1,0:T(8,128)(2,1)S(1)} %copy-done.2, bf16[2,1024,1024]{2,1,0:T(8,128)(2,1)S(1)} %copy-done.1), custom_call_target="tpu_custom_call" | custom-call | flops 671088640 | bytes 8781824 | tf_op jit(solution)/shard_map/pallas_call | solution.py:263
  64.7 1.0 %collective-permute-done.17.arrived_ref = bf16[64,1024]{1,0:T(8,128)(2,1)S(1)} collective-permute-done((bf16[64,1024]{1,0:T(8,128)(2,1)S(1)}, bf16[64,1024]{1,0:T(8,128)(2,1)S(1)}, u32[]{:S(2)}, u32[]{:S(2)}) %collective-permute-start.17) | collective-permute-done | bytes 131104 | tf_op jit(solution)/shard_map/ppermute | solution.py:28
  65.8 1.4 %shard_map.61 = (f32[2,64,1024]{2,1,0:T(8,128)S(1)}, bf16[2,64,1024]{2,1,0:T(8,128)(2,1)S(1)}, bf16[64,1024]{1,0:T(8,128)(2,1)S(1)}, bf16[64,1024]{1,0:T(8,128)(2,1)S(1)}) custom-call(s32[1]{0:T(128)} %bitcast.1.at_ref, f32[2]{0:T(128)S(1)} %pad_maximum_fusion.shift_ref, f32[2,64,1024]{2,1,0:T(8,128)S(1)} %shard_map.60.sum_in_ref, ...), custom_call_target="tpu_custom_call" | custom-call | flops 268435456 | bytes 5898240 | tf_op jit(solution)/shard_map/pallas_call | solution.py:263
  67.2 0.6 collective-permute-start.18
  67.8 1.3 %collective-permute-start.19 = (bf16[64,1024]{1,0:T(8,128)(2,1)S(1)}, bf16[64,1024]{1,0:T(8,128)(2,1)S(1)}, u32[]{:S(2)}, u32[]{:S(2)}) collective-permute-start(bf16[64,1024]{1,0:T(8,128)(2,1)S(1)} %get-tuple-element.74), channel_id=1, source_target_pairs={{0,8},{1,2},{2,1},{3,4},{4,3},{5,6},{6,5},{7,15},{8,0},{9,10},{10,... | collective-permute-start | bytes 393224 | tf_op jit(solution)/shard_map/ppermute | solution.py:28
  69.1 2.6 %shard_map.62.sum_in_ref = f32[2,64,1024]{2,1,0:T(8,128)S(1)} custom-call(s32[1]{0:T(128)} %bitcast.1.at_ref, bf16[2,64,1024]{2,1,0:T(8,128)(2,1)S(1)} %get-tuple-element.72.rounded_ref, bf16[64,1024]{1,0:T(8,128)(2,1)S(1)} %collective-permute-done.18.arrived_ref, bf16[2,1024,1024]{2,1,0:T(8,128)(2,1)S(1)} %copy-done.2, bf16[2,1024,1024]{2,1,0:T(8,128)(2,1)S(1)} %copy-done.1), custom_call_target="tpu_custom_call" | custom-call | flops 671088640 | bytes 8781824 | tf_op jit(solution)/shard_map/pallas_call | solution.py:263
  71.7 1.0 %collective-permute-done.19.arrived_ref = bf16[64,1024]{1,0:T(8,128)(2,1)S(1)} collective-permute-done((bf16[64,1024]{1,0:T(8,128)(2,1)S(1)}, bf16[64,1024]{1,0:T(8,128)(2,1)S(1)}, u32[]{:S(2)}, u32[]{:S(2)}) %collective-permute-start.19) | collective-permute-done | bytes 131104 | tf_op jit(solution)/shard_map/ppermute | solution.py:28
  72.8 1.2 %shard_map.63 = (f32[2,64,1024]{2,1,0:T(8,128)S(1)}, bf16[2,64,1024]{2,1,0:T(8,128)(2,1)S(1)}, f32[64,64]{1,0:T(8,128)S(1)}) custom-call(s32[1]{0:T(128)} %bitcast.1.at_ref, f32[2]{0:T(128)S(1)} %pad_maximum_fusion.shift_ref, f32[2,64,1024]{2,1,0:T(8,128)S(1)} %shard_map.62.sum_in_ref, bf16[64,1024]{1,0:T(8,128)(2,1)S(1)} %collective-permute-done.19.arrived_ref, ...), custom_call_target="tpu_custom_call" | custom-call | flops 268435456 | bytes 5898240 | tf_op jit(solution)/shard_map/pallas_call | solution.py:263
  74.0 1.4 %collective-permute-start.20 = (bf16[2,64,1024]{2,1,0:T(8,128)(2,1)S(1)}, bf16[2,64,1024]{2,1,0:T(8,128)(2,1)S(1)}, u32[]{:S(2)}, u32[]{:S(2)}) collective-permute-start(bf16[2,64,1024]{2,1,0:T(8,128)(2,1)S(1)} %get-tuple-element.77.rounded_ref), channel_id=1, source_target_pairs={{0,8},{8,16},{16,24},{24,0},{1,9},{9,17},{17,25},{25,1},{2,10},{10... | collective-permute-start | bytes 786440 | tf_op jit(solution)/shard_map/ppermute | solution.py:33
  75.4 1.6 %collective-permute-start.21 = (bf16[2,16,1024]{2,1,0:T(8,128)(2,1)S(1)}, bf16[2,16,1024]{2,1,0:T(8,128)(2,1)S(1)}, u32[]{:S(2)}, u32[]{:S(2)}) collective-permute-start(bf16[2,16,1024]{2,1,0:T(8,128)(2,1)S(1)} %slice.11), channel_id=1, source_target_pairs={{0,24},{8,0},{16,8},{24,16},{1,25},{9,1},{17,9},{25,17},{2,26},{10... | collective-permute-start | bytes 196616 | tf_op jit(solution)/shard_map/ppermute | solution.py:33
  77.0 8.2 %collective-permute-done.21.above_ref.refs_6_ = bf16[2,16,1024]{2,1,0:T(8,128)(2,1)S(1)} collective-permute-done((bf16[2,16,1024]{2,1,0:T(8,128)(2,1)S(1)}, bf16[2,16,1024]{2,1,0:T(8,128)(2,1)S(1)}, u32[]{:S(2)}, u32[]{:S(2)}) %collective-permute-start.21) | collective-permute-done | bytes 65568 | tf_op jit(solution)/shard_map/ppermute | solution.py:33
  85.2 0.4 shard_map.64
  85.7 1.2 %collective-permute-done.22 = f32[64,176]{1,0:T(8,128)S(1)} collective-permute-done((f32[64,176]{1,0:T(8,128)S(1)}, f32[64,176]{1,0:T(8,128)S(1)}, u32[]{:S(2)}, u32[]{:S(2)}) %collective-permute-start.22) | collective-permute-done | bytes 45088 | tf_op jit(solution)/shard_map/ppermute | solution.py:40
  87.0 2.2 %collective-permute-start.24 = (f32[64,176]{1,0:T(8,128)S(1)}, f32[64,176]{1,0:T(8,128)S(1)}, u32[]{:S(2)}, u32[]{:S(2)}) collective-permute-start(f32[64,176]{1,0:T(8,128)S(1)} %add.12.refs_0_), channel_id=1, source_target_pairs={{0,4},{1,5},{2,6},{3,7},{4,0},{5,1},{6,2},{7,3},{8,12},{9,13},{10,... | collective-permute-start | bytes 135176 | tf_op jit(solution)/shard_map/ppermute | solution.py:46
  89.2 2.2 %collective-permute-start.23 = (f32[64,176]{1,0:T(8,128)S(1)}, f32[64,176]{1,0:T(8,128)S(1)}, u32[]{:S(2)}, u32[]{:S(2)}) collective-permute-start(f32[64,176]{1,0:T(8,128)S(1)} %add.12.refs_0_), channel_id=1, source_target_pairs={{0,2},{1,3},{2,0},{3,1},{4,6},{5,7},{6,4},{7,5},{8,10},{9,11},{10,... | collective-permute-start | bytes 135176 | tf_op jit(solution)/shard_map/ppermute | solution.py:46
  91.4 2.4 %collective-permute-done.25.refs_3_ = f32[64,176]{1,0:T(8,128)S(1)} collective-permute-done((f32[64,176]{1,0:T(8,128)S(1)}, f32[64,176]{1,0:T(8,128)S(1)}, u32[]{:S(2)}, u32[]{:S(2)}) %collective-permute-start.25) | collective-permute-done | bytes 45088 | tf_op jit(solution)/shard_map/ppermute | solution.py:46
  93.8 1.9 %collective-permute-done.24.refs_2_ = f32[64,176]{1,0:T(8,128)S(1)} collective-permute-done((f32[64,176]{1,0:T(8,128)S(1)}, f32[64,176]{1,0:T(8,128)S(1)}, u32[]{:S(2)}, u32[]{:S(2)}) %collective-permute-start.24) | collective-permute-done | bytes 45088 | tf_op jit(solution)/shard_map/ppermute | solution.py:46
  95.6 5.7 %shard_map.65 = f32[64,2,1024]{2,1,0:T(2,128)} custom-call(s32[1]{0:T(128)} %bitcast.cut_ref, f32[64,176]{1,0:T(8,128)S(1)} %add.12.refs_0_, f32[64,176]{1,0:T(8,128)S(1)} %collective-permute-done.23.refs_1_, f32[64,176]{1,0:T(8,128)S(1)} %collective-permute-done.24.refs_2_, f32[64,176]{1,0:T(8,128)S(1)} %collective-permute-done.25.refs_3_, ...), custom_call_target="tpu_custom_call" | custom-call | bytes 1032192 | tf_op jit(solution)/shard_map/pallas_call | solution.py:263
  (23 shorter events, 0.2 us)
Async XLA Ops:
  0.0 7.6 %copy-start.4 = (s32[1,2]{1,0:T(1,128)S(1)}, s32[1,2]{1,0:T(1,128)}, u32[]{:S(2)}) copy-start(s32[1,2]{1,0:T(1,128)} %param.7) | copy-start | bytes 28
  0.0 2.2 %copy-start = (bf16[2,1024,1024]{2,1,0:T(8,128)(2,1)S(1)}, bf16[2,1024,1024]{2,1,0:T(8,128)(2,1)}, u32[]{:S(2)}) copy-start(bf16[2,1024,1024]{2,1,0:T(8,128)(2,1)} %couplings_ref.33) | copy-start | bytes 12582916
  2.2 1.0 %copy-start.3 = (f32[1,64,2,1024]{3,2,1,0:T(2,128)S(1)}, f32[1,64,2,1024]{3,2,1,0:T(2,128)}, u32[]{:S(2)}) copy-start(f32[1,64,2,1024]{3,2,1,0:T(2,128)} %param.4) | copy-start | bytes 1572868
  3.2 6.3 %copy-start.1 = (bf16[2,1024,1024]{2,1,0:T(8,128)(2,1)S(1)}, bf16[2,1024,1024]{2,1,0:T(8,128)(2,1)}, u32[]{:S(2)}) copy-start(bf16[2,1024,1024]{2,1,0:T(8,128)(2,1)} %couplings_ref.33) | copy-start | bytes 12582916
  4.5 5.0 %collective-permute-start = (bf16[64,1024]{1,0:T(8,128)(2,1)S(1)}, bf16[64,1024]{1,0:T(8,128)(2,1)S(1)}, u32[]{:S(2)}, u32[]{:S(2)}) collective-permute-start(bf16[64,1024]{1,0:T(8,128)(2,1)S(1)} %get-tuple-element.43), channel_id=1, source_target_pairs={{0,1},{1,0},{2,3},{3,2},{4,5},{5,4},{6,7},{7,6},{8,9},{9,8},{10,11... | collective-permute-start | bytes 393224 | tf_op jit(solution)/shard_map/ppermute | solution.py:28
  5.0 9.3 %collective-permute-start.1 = (bf16[64,1024]{1,0:T(8,128)(2,1)S(1)}, bf16[64,1024]{1,0:T(8,128)(2,1)S(1)}, u32[]{:S(2)}, u32[]{:S(2)}) collective-permute-start(bf16[64,1024]{1,0:T(8,128)(2,1)S(1)} %get-tuple-element.44), channel_id=1, source_target_pairs={{0,8},{1,2},{2,1},{3,4},{4,3},{5,6},{6,5},{7,15},{8,0},{9,10},{10,... | collective-permute-start | bytes 393224 | tf_op jit(solution)/shard_map/ppermute | solution.py:28
  9.5 2.2 %copy-start.2 = (bf16[2,1024,1024]{2,1,0:T(8,128)(2,1)S(1)}, bf16[2,1024,1024]{2,1,0:T(8,128)(2,1)}, u32[]{:S(2)}) copy-start(bf16[2,1024,1024]{2,1,0:T(8,128)(2,1)} %diag_ref.15) | copy-start | bytes 12582916
  15.4 1.8 %collective-permute-start.2 = (bf16[64,1024]{1,0:T(8,128)(2,1)S(1)}, bf16[64,1024]{1,0:T(8,128)(2,1)S(1)}, u32[]{:S(2)}, u32[]{:S(2)}) collective-permute-start(bf16[64,1024]{1,0:T(8,128)(2,1)S(1)} %get-tuple-element.47), channel_id=1, source_target_pairs={{0,1},{1,0},{2,3},{3,2},{4,5},{5,4},{6,7},{7,6},{8,9},{9,8},{10,11... | collective-permute-start | bytes 393224 | tf_op jit(solution)/shard_map/ppermute | solution.py:28
  15.8 5.0 %collective-permute-start.3 = (bf16[64,1024]{1,0:T(8,128)(2,1)S(1)}, bf16[64,1024]{1,0:T(8,128)(2,1)S(1)}, u32[]{:S(2)}, u32[]{:S(2)}) collective-permute-start(bf16[64,1024]{1,0:T(8,128)(2,1)S(1)} %get-tuple-element.48), channel_id=1, source_target_pairs={{0,8},{1,2},{2,1},{3,4},{4,3},{5,6},{6,5},{7,15},{8,0},{9,10},{10,... | collective-permute-start | bytes 393224 | tf_op jit(solution)/shard_map/ppermute | solution.py:28
  21.9 2.1 %collective-permute-start.4 = (bf16[64,1024]{1,0:T(8,128)(2,1)S(1)}, bf16[64,1024]{1,0:T(8,128)(2,1)S(1)}, u32[]{:S(2)}, u32[]{:S(2)}) collective-permute-start(bf16[64,1024]{1,0:T(8,128)(2,1)S(1)} %get-tuple-element.51), channel_id=1, source_target_pairs={{0,1},{1,0},{2,3},{3,2},{4,5},{5,4},{6,7},{7,6},{8,9},{9,8},{10,11... | collective-permute-start | bytes 393224 | tf_op jit(solution)/shard_map/ppermute | solution.py:28
  22.7 5.0 %collective-permute-start.5 = (bf16[64,1024]{1,0:T(8,128)(2,1)S(1)}, bf16[64,1024]{1,0:T(8,128)(2,1)S(1)}, u32[]{:S(2)}, u32[]{:S(2)}) collective-permute-start(bf16[64,1024]{1,0:T(8,128)(2,1)S(1)} %get-tuple-element.52), channel_id=1, source_target_pairs={{0,8},{1,2},{2,1},{3,4},{4,3},{5,6},{6,5},{7,15},{8,0},{9,10},{10,... | collective-permute-start | bytes 393224 | tf_op jit(solution)/shard_map/ppermute | solution.py:28
  28.8 1.9 %collective-permute-start.6 = (bf16[64,1024]{1,0:T(8,128)(2,1)S(1)}, bf16[64,1024]{1,0:T(8,128)(2,1)S(1)}, u32[]{:S(2)}, u32[]{:S(2)}) collective-permute-start(bf16[64,1024]{1,0:T(8,128)(2,1)S(1)} %get-tuple-element.55), channel_id=1, source_target_pairs={{0,1},{1,0},{2,3},{3,2},{4,5},{5,4},{6,7},{7,6},{8,9},{9,8},{10,11... | collective-permute-start | bytes 393224 | tf_op jit(solution)/shard_map/ppermute | solution.py:28
  29.4 5.0 %collective-permute-start.7 = (bf16[64,1024]{1,0:T(8,128)(2,1)S(1)}, bf16[64,1024]{1,0:T(8,128)(2,1)S(1)}, u32[]{:S(2)}, u32[]{:S(2)}) collective-permute-start(bf16[64,1024]{1,0:T(8,128)(2,1)S(1)} %get-tuple-element.56), channel_id=1, source_target_pairs={{0,8},{1,2},{2,1},{3,4},{4,3},{5,6},{6,5},{7,15},{8,0},{9,10},{10,... | collective-permute-start | bytes 393224 | tf_op jit(solution)/shard_map/ppermute | solution.py:28
  36.3 1.4 %collective-permute-start.8 = (f32[64,64]{1,0:T(8,128)S(1)}, f32[64,64]{1,0:T(8,128)S(1)}, u32[]{:S(2)}, u32[]{:S(2)}) collective-permute-start(f32[64,64]{1,0:T(8,128)S(1)} %get-tuple-element.58), channel_id=1, source_target_pairs={{0,1},{1,0},{2,3},{3,2},{4,5},{5,4},{6,7},{7,6},{8,9},{9,8},{10,11... | collective-permute-start | bytes 49160 | tf_op jit(solution)/shard_map/ppermute | solution.py:40
  37.7 6.1 %collective-permute-start.11 = (f32[64,64]{1,0:T(8,128)S(1)}, f32[64,64]{1,0:T(8,128)S(1)}, u32[]{:S(2)}, u32[]{:S(2)}) collective-permute-start(f32[64,64]{1,0:T(8,128)S(1)} %add.11.refs_0_), channel_id=1, source_target_pairs={{0,6},{1,7},{2,4},{3,5},{4,2},{5,3},{6,0},{7,1},{8,14},{9,15},{10,... | collective-permute-start | bytes 49160 | tf_op jit(solution)/shard_map/ppermute | solution.py:46
  38.2 5.6 %collective-permute-start.10 = (f32[64,64]{1,0:T(8,128)S(1)}, f32[64,64]{1,0:T(8,128)S(1)}, u32[]{:S(2)}, u32[]{:S(2)}) collective-permute-start(f32[64,64]{1,0:T(8,128)S(1)} %add.11.refs_0_), channel_id=1, source_target_pairs={{0,4},{1,5},{2,6},{3,7},{4,0},{5,1},{6,2},{7,3},{8,12},{9,13},{10,... | collective-permute-start | bytes 49160 | tf_op jit(solution)/shard_map/ppermute | solution.py:46
  39.8 4.4 %collective-permute-start.9 = (f32[64,64]{1,0:T(8,128)S(1)}, f32[64,64]{1,0:T(8,128)S(1)}, u32[]{:S(2)}, u32[]{:S(2)}) collective-permute-start(f32[64,64]{1,0:T(8,128)S(1)} %add.11.refs_0_), channel_id=1, source_target_pairs={{0,2},{1,3},{2,0},{3,1},{4,6},{5,7},{6,4},{7,5},{8,10},{9,11},{10,... | collective-permute-start | bytes 49160 | tf_op jit(solution)/shard_map/ppermute | solution.py:46
  46.9 1.5 %collective-permute-start.12 = (bf16[64,1024]{1,0:T(8,128)(2,1)S(1)}, bf16[64,1024]{1,0:T(8,128)(2,1)S(1)}, u32[]{:S(2)}, u32[]{:S(2)}) collective-permute-start(bf16[64,1024]{1,0:T(8,128)(2,1)S(1)} %get-tuple-element.61), channel_id=1, source_target_pairs={{0,1},{1,0},{2,3},{3,2},{4,5},{5,4},{6,7},{7,6},{8,9},{9,8},{10,11... | collective-permute-start | bytes 393224 | tf_op jit(solution)/shard_map/ppermute | solution.py:28
  47.0 5.0 %collective-permute-start.13 = (bf16[64,1024]{1,0:T(8,128)(2,1)S(1)}, bf16[64,1024]{1,0:T(8,128)(2,1)S(1)}, u32[]{:S(2)}, u32[]{:S(2)}) collective-permute-start(bf16[64,1024]{1,0:T(8,128)(2,1)S(1)} %get-tuple-element.62), channel_id=1, source_target_pairs={{0,8},{1,2},{2,1},{3,4},{4,3},{5,6},{6,5},{7,15},{8,0},{9,10},{10,... | collective-permute-start | bytes 393224 | tf_op jit(solution)/shard_map/ppermute | solution.py:28
  53.1 2.3 %collective-permute-start.14 = (bf16[64,1024]{1,0:T(8,128)(2,1)S(1)}, bf16[64,1024]{1,0:T(8,128)(2,1)S(1)}, u32[]{:S(2)}, u32[]{:S(2)}) collective-permute-start(bf16[64,1024]{1,0:T(8,128)(2,1)S(1)} %get-tuple-element.65), channel_id=1, source_target_pairs={{0,1},{1,0},{2,3},{3,2},{4,5},{5,4},{6,7},{7,6},{8,9},{9,8},{10,11... | collective-permute-start | bytes 393224 | tf_op jit(solution)/shard_map/ppermute | solution.py:28
  54.1 5.0 %collective-permute-start.15 = (bf16[64,1024]{1,0:T(8,128)(2,1)S(1)}, bf16[64,1024]{1,0:T(8,128)(2,1)S(1)}, u32[]{:S(2)}, u32[]{:S(2)}) collective-permute-start(bf16[64,1024]{1,0:T(8,128)(2,1)S(1)} %get-tuple-element.66), channel_id=1, source_target_pairs={{0,8},{1,2},{2,1},{3,4},{4,3},{5,6},{6,5},{7,15},{8,0},{9,10},{10,... | collective-permute-start | bytes 393224 | tf_op jit(solution)/shard_map/ppermute | solution.py:28
  60.2 2.0 %collective-permute-start.16 = (bf16[64,1024]{1,0:T(8,128)(2,1)S(1)}, bf16[64,1024]{1,0:T(8,128)(2,1)S(1)}, u32[]{:S(2)}, u32[]{:S(2)}) collective-permute-start(bf16[64,1024]{1,0:T(8,128)(2,1)S(1)} %get-tuple-element.69), channel_id=1, source_target_pairs={{0,1},{1,0},{2,3},{3,2},{4,5},{5,4},{6,7},{7,6},{8,9},{9,8},{10,11... | collective-permute-start | bytes 393224 | tf_op jit(solution)/shard_map/ppermute | solution.py:28
  60.8 5.0 %collective-permute-start.17 = (bf16[64,1024]{1,0:T(8,128)(2,1)S(1)}, bf16[64,1024]{1,0:T(8,128)(2,1)S(1)}, u32[]{:S(2)}, u32[]{:S(2)}) collective-permute-start(bf16[64,1024]{1,0:T(8,128)(2,1)S(1)} %get-tuple-element.70), channel_id=1, source_target_pairs={{0,8},{1,2},{2,1},{3,4},{4,3},{5,6},{6,5},{7,15},{8,0},{9,10},{10,... | collective-permute-start | bytes 393224 | tf_op jit(solution)/shard_map/ppermute | solution.py:28
  67.2 2.0 %collective-permute-start.18 = (bf16[64,1024]{1,0:T(8,128)(2,1)S(1)}, bf16[64,1024]{1,0:T(8,128)(2,1)S(1)}, u32[]{:S(2)}, u32[]{:S(2)}) collective-permute-start(bf16[64,1024]{1,0:T(8,128)(2,1)S(1)} %get-tuple-element.73), channel_id=1, source_target_pairs={{0,1},{1,0},{2,3},{3,2},{4,5},{5,4},{6,7},{7,6},{8,9},{9,8},{10,11... | collective-permute-start | bytes 393224 | tf_op jit(solution)/shard_map/ppermute | solution.py:28
  67.8 5.0 %collective-permute-start.19 = (bf16[64,1024]{1,0:T(8,128)(2,1)S(1)}, bf16[64,1024]{1,0:T(8,128)(2,1)S(1)}, u32[]{:S(2)}, u32[]{:S(2)}) collective-permute-start(bf16[64,1024]{1,0:T(8,128)(2,1)S(1)} %get-tuple-element.74), channel_id=1, source_target_pairs={{0,8},{1,2},{2,1},{3,4},{4,3},{5,6},{6,5},{7,15},{8,0},{9,10},{10,... | collective-permute-start | bytes 393224 | tf_op jit(solution)/shard_map/ppermute | solution.py:28
  74.0 11.2 %collective-permute-start.20 = (bf16[2,64,1024]{2,1,0:T(8,128)(2,1)S(1)}, bf16[2,64,1024]{2,1,0:T(8,128)(2,1)S(1)}, u32[]{:S(2)}, u32[]{:S(2)}) collective-permute-start(bf16[2,64,1024]{2,1,0:T(8,128)(2,1)S(1)} %get-tuple-element.77.rounded_ref), channel_id=1, source_target_pairs={{0,8},{8,16},{16,24},{24,0},{1,9},{9,17},{17,25},{25,1},{2,10},{10... | collective-permute-start | bytes 786440 | tf_op jit(solution)/shard_map/ppermute | solution.py:33
  75.4 9.8 %collective-permute-start.21 = (bf16[2,16,1024]{2,1,0:T(8,128)(2,1)S(1)}, bf16[2,16,1024]{2,1,0:T(8,128)(2,1)S(1)}, u32[]{:S(2)}, u32[]{:S(2)}) collective-permute-start(bf16[2,16,1024]{2,1,0:T(8,128)(2,1)S(1)} %slice.11), channel_id=1, source_target_pairs={{0,24},{8,0},{16,8},{24,16},{1,25},{9,1},{17,9},{25,17},{2,26},{10... | collective-permute-start | bytes 196616 | tf_op jit(solution)/shard_map/ppermute | solution.py:33
  85.6 1.3 %collective-permute-start.22 = (f32[64,176]{1,0:T(8,128)S(1)}, f32[64,176]{1,0:T(8,128)S(1)}, u32[]{:S(2)}, u32[]{:S(2)}) collective-permute-start(f32[64,176]{1,0:T(8,128)S(1)} %shard_map.64), channel_id=1, source_target_pairs={{0,1},{1,0},{2,3},{3,2},{4,5},{5,4},{6,7},{7,6},{8,9},{9,8},{10,11... | collective-permute-start | bytes 135176 | tf_op jit(solution)/shard_map/ppermute | solution.py:40
  86.9 6.8 %collective-permute-start.25 = (f32[64,176]{1,0:T(8,128)S(1)}, f32[64,176]{1,0:T(8,128)S(1)}, u32[]{:S(2)}, u32[]{:S(2)}) collective-permute-start(f32[64,176]{1,0:T(8,128)S(1)} %add.12.refs_0_), channel_id=1, source_target_pairs={{0,6},{1,7},{2,4},{3,5},{4,2},{5,3},{6,0},{7,1},{8,14},{9,15},{10,... | collective-permute-start | bytes 135176 | tf_op jit(solution)/shard_map/ppermute | solution.py:46
  87.0 8.6 %collective-permute-start.24 = (f32[64,176]{1,0:T(8,128)S(1)}, f32[64,176]{1,0:T(8,128)S(1)}, u32[]{:S(2)}, u32[]{:S(2)}) collective-permute-start(f32[64,176]{1,0:T(8,128)S(1)} %add.12.refs_0_), channel_id=1, source_target_pairs={{0,4},{1,5},{2,6},{3,7},{4,0},{5,1},{6,2},{7,3},{8,12},{9,13},{10,... | collective-permute-start | bytes 135176 | tf_op jit(solution)/shard_map/ppermute | solution.py:46
  89.2 6.4 %collective-permute-start.23 = (f32[64,176]{1,0:T(8,128)S(1)}, f32[64,176]{1,0:T(8,128)S(1)}, u32[]{:S(2)}, u32[]{:S(2)}) collective-permute-start(f32[64,176]{1,0:T(8,128)S(1)} %add.12.refs_0_), channel_id=1, source_target_pairs={{0,2},{1,3},{2,0},{3,1},{4,6},{5,7},{6,4},{7,5},{8,10},{9,11},{10,... | collective-permute-start | bytes 135176 | tf_op jit(solution)/shard_map/ppermute | solution.py:46
